TPU v7x, 128 devices: a whole 4x4x4 slice. The times are simulated.
128 devices in a mesh: dp: 8 (over y, core), expert: 16 (over z, x).
Axes of the slice: x: 4, y: 4, z: 4, core: 2. Of those that a mesh axis runs over, the one named last changes fastest.
Arguments:
- hidden: bfloat16 [2, 2048, 2048], P(None, ('dp', 'expert')), may hold values from -6 to 6
- q_self: bfloat16 [2, 2048, 2048], P(None, ('dp', 'expert')), may hold values from -60 to 60
- k_new: bfloat16 [2, 2048, 2048], P(None, ('dp', 'expert')), may hold values from -6 to 6
- v_new: bfloat16 [2, 2048, 2048], P(None, ('dp', 'expert')), may hold values from -6 to 6
- q_cross: bfloat16 [2, 2048, 2048], P(None, ('dp', 'expert')), may hold values from -40 to 40
- cache_keys: bfloat16 [2048, 64, 2048], P(('dp', 'expert')), may hold values from -6 to 6
- cache_values: bfloat16 [2048, 64, 2048], P(('dp', 'expert')), may hold values from -6 to 6
- cross_keys: bfloat16 [512, 256, 2048], P(('dp', 'expert')), may hold values from -127 to 127, as said below
- cross_values: bfloat16 [512, 256, 2048], P(('dp', 'expert')), may hold values from -127 to 127, as said below
- key_scale: float32 [512, 16], P(('dp', 'expert')), may hold values from 0.01 to 0.02
- value_scale: float32 [512, 16], P(('dp', 'expert')), may hold values from 0.005 to 0.03
- parents: int32 [2, 2048], P(None, ('dp', 'expert')), may hold values from 0 to 2047, as said below
- expert_ids: int32 [2, 2048, 2], P(None, ('dp', 'expert')), may hold values from 0 to 15, all different within a row; in each aligned block of 16 rows (0 to 15, 16 to 31, ..., all dimensions but the last counted through in order) at most 4 rows name the same one
- norm_gain: float32 [2048], replicated, may hold values from 0.1 to 1.9
- router: bfloat16 [2048, 16], replicated, may hold values from -0.125 to 0.125
- w_in: bfloat16 [16, 2048, 8192], P('expert', None, 'dp'), may hold values from -0.125 to 0.125
- w_out: bfloat16 [16, 8192, 2048], P('expert', 'dp'), may hold values from -0.0625 to 0.0625
Outputs:
- mixed: bfloat16 [2, 2048, 2048], P(None, ('dp', 'expert'))
Inputs may be any that keep to these rules, and one draw needn't show every extreme that they name: `parents`: in each step, on the rows of each device exactly 4 beams take a parent among the rows of the previous device along dp+expert (the last device for the first); every other beam takes a beam of its own sentence. `expert_ids`: in each step, no expert is named by more than 4 of the rows of one device. `cross_keys`: whole numbers. `cross_values`: whole numbers.
All inputs are finite; a program needn't handle non-finite values.
Results may differ from a plain program's by a relative error of at most 0.012.
Values may be sent and summed in bfloat16 or wider, within the bound.
A program may use at most 192 MiB of HBM per device.

v0:
```python
import math

import jax
import jax.numpy as jnp
from jax import lax
from jax.sharding import PartitionSpec as P

epsilon = 1e-05


def passed_along(value, axis, steps):
    count = lax.axis_size(axis)
    pairs = [(source, (source + steps) % count) for source in range(count)]
    return lax.ppermute(value, axis, pairs)


def soft_weights(scores):
    top_score = jnp.max(scores, axis=-1, keepdims=True)
    weights = jnp.exp(scores - top_score)
    return (weights / jnp.sum(weights, axis=-1, keepdims=True)).astype(jnp.bfloat16)


def reorder(key_rows, value_rows, parent, own_start, prev_start):
    row_count = key_rows.shape[0]
    in_prev = (parent >= prev_start) & (parent < prev_start + row_count)
    own_index = jnp.clip(parent - own_start, 0, row_count - 1)
    own_keys = jnp.take(key_rows, own_index, axis=0)
    own_values = jnp.take(value_rows, own_index, axis=0)
    row_mask = in_prev[:, None, None]
    prev_keys, prev_values = passed_along((key_rows, value_rows), ("dp", "expert"), 1)
    prev_index = jnp.clip(parent - prev_start, 0, row_count - 1)
    far_keys = jnp.take(prev_keys, prev_index, axis=0)
    far_values = jnp.take(prev_values, prev_index, axis=0)
    return (jnp.where(row_mask, far_keys, own_keys), jnp.where(row_mask, far_values, own_values))


def experts_apply(normed, chosen_ids, w_in, w_out):
    stack_size, row_count, top_count = chosen_ids.shape
    width = normed.shape[2]
    expert_count = lax.axis_size("expert") * w_in.shape[0]
    capacity = max(2, 2 * row_count * top_count // expert_count)
    picked_ids = chosen_ids.reshape(stack_size, row_count * top_count)
    one_hot = (
        picked_ids[:, :, None] == jnp.arange(expert_count, dtype=jnp.int32)[None, None, :]
    ).astype(jnp.int32)
    before = jnp.cumsum(one_hot, axis=1) - one_hot
    slot_pos = jnp.sum(before * one_hot, axis=2)
    column = (
        picked_ids * (stack_size * capacity)
        + jnp.arange(stack_size, dtype=jnp.int32)[:, None] * capacity
        + slot_pos
    )
    columns = expert_count * stack_size * capacity
    dispatch = (
        column.reshape(-1)[:, None] == jnp.arange(columns, dtype=jnp.int32)[None, :]
    ).astype(jnp.bfloat16)
    sources = jnp.repeat(normed.reshape(stack_size * row_count, width), top_count, axis=0)
    outgoing = jnp.einsum(
        "pc,pd->cd", dispatch, sources, preferred_element_type=jnp.float32
    ).astype(jnp.bfloat16)
    outgoing = outgoing.reshape(expert_count, stack_size * capacity, width)
    arrived = lax.all_to_all(outgoing, "expert", split_axis=0, concat_axis=0, tiled=True)
    arrived = arrived.reshape(lax.axis_size("expert"), w_in.shape[0], stack_size * capacity, width)
    units = jax.nn.relu(
        jnp.einsum(
            "secd,edf->secf",
            lax.all_gather(arrived, "dp", axis=0, tiled=True),
            w_in,
            preferred_element_type=jnp.float32,
        )
    ).astype(jnp.bfloat16)
    partial_out = jnp.einsum(
        "secf,efd->secd", units, w_out, preferred_element_type=jnp.float32
    ).astype(jnp.bfloat16)
    summed = (
        lax.psum_scatter(partial_out, "dp", scatter_dimension=0, tiled=True)
        .astype(jnp.float32)
        .astype(jnp.bfloat16)
    )
    returned = lax.all_to_all(
        summed.reshape(expert_count, stack_size * capacity, width),
        "expert",
        split_axis=0,
        concat_axis=0,
        tiled=True,
    )
    gathered = jnp.dot(
        dispatch, returned.reshape(columns, width), preferred_element_type=jnp.float32
    )
    return gathered.reshape(stack_size, row_count, top_count, width)


def finish(residual, normed, chosen_ids, router, w_in, w_out):
    expert_count = router.shape[1]
    logits = jnp.einsum("srd,de->sre", normed, router, preferred_element_type=jnp.float32)
    match_table = (
        chosen_ids[:, :, :, None] == jnp.arange(expert_count, dtype=jnp.int32)[None, None, None, :]
    )
    chosen = jnp.sum(jnp.where(match_table, logits[:, :, None, :], 0.0), axis=3)
    first_gate = jax.nn.sigmoid(chosen[:, :, 0] - chosen[:, :, 1])
    gate_mix = jnp.stack([first_gate, 1.0 - first_gate], axis=2)
    expert_out = experts_apply(normed, chosen_ids, w_in, w_out)
    return (residual + jnp.sum(gate_mix[:, :, :, None] * expert_out, axis=2)).astype(jnp.bfloat16)


def shards(
    hidden,
    q_self,
    k_new,
    v_new,
    q_cross,
    cache_keys,
    cache_values,
    cross_keys,
    cross_values,
    key_scale,
    value_scale,
    parents,
    expert_ids,
    norm_gain,
    router,
    w_in,
    w_out,
):
    step_count = hidden.shape[0]
    row_count = hidden.shape[1]
    width = hidden.shape[2]
    head_count = key_scale.shape[1]
    head_size = width // head_count
    sentences = cross_keys.shape[0]
    beam_count = row_count // sentences
    source_len = cross_keys.shape[1]
    dev_count = lax.axis_size(("dp", "expert"))
    position = lax.axis_index(("dp", "expert"))
    own_start = position * row_count
    prev_start = (position + dev_count - 1) % dev_count * row_count
    key_deq = (
        cross_keys.reshape(sentences, source_len, head_count, head_size).astype(jnp.float32)
        * key_scale[:, None, :, None]
    ).astype(jnp.bfloat16)
    value_deq = (
        cross_values.reshape(sentences, source_len, head_count, head_size).astype(jnp.float32)
        * value_scale[:, None, :, None]
    ).astype(jnp.bfloat16)
    key_cache, value_cache = (cache_keys, cache_values)
    pieces = []
    for step_index in range(step_count):
        attention_key_cache = key_cache
        attention_value_cache = value_cache
        attention_key_cache, attention_value_cache = reorder(
            attention_key_cache, attention_value_cache, parents[step_index], own_start, prev_start
        )
        attention_key_cache = jnp.concatenate(
            [attention_key_cache, k_new[step_index][:, None, :]], axis=1
        )
        attention_value_cache = jnp.concatenate(
            [attention_value_cache, v_new[step_index][:, None, :]], axis=1
        )
        length = attention_key_cache.shape[1]
        query = q_self[step_index].reshape(row_count, head_count, head_size)
        scores = jnp.einsum(
            "rhe,rlhe->rhl",
            query,
            attention_key_cache.reshape(row_count, length, head_count, head_size),
            preferred_element_type=jnp.float32,
        ) / math.sqrt(head_size)
        prob_bf = soft_weights(scores)
        self_out = jnp.einsum(
            "rhl,rlhe->rhe",
            prob_bf,
            attention_value_cache.reshape(row_count, length, head_count, head_size),
            preferred_element_type=jnp.float32,
        ).reshape(row_count, width)
        cross_q = q_cross[step_index].reshape(sentences, beam_count, head_count, head_size)
        cross_scores = jnp.einsum(
            "sbhe,slhe->sbhl", cross_q, key_deq, preferred_element_type=jnp.float32
        ) / math.sqrt(head_size)
        cross_prob = soft_weights(cross_scores)
        cross_out = jnp.einsum(
            "sbhl,slhe->sbhe", cross_prob, value_deq, preferred_element_type=jnp.float32
        ).reshape(row_count, width)
        residual = hidden[step_index].astype(jnp.float32) + self_out + cross_out
        average = jnp.mean(residual, axis=1, keepdims=True)
        centered = residual - average
        variance = jnp.mean(centered * centered, axis=1, keepdims=True)
        normed = (centered * lax.rsqrt(variance + epsilon) * norm_gain[None, :]).astype(
            jnp.bfloat16
        )
        key_cache, value_cache, residual, normed = (
            attention_key_cache,
            attention_value_cache,
            residual,
            normed,
        )
        pieces.append(
            finish(residual[None], normed[None], expert_ids[step_index][None], router, w_in, w_out)
        )
    outputs = jnp.concatenate(pieces, axis=0)
    return outputs


def solution(mesh):
    in_specs = (
        P(None, ("dp", "expert"), None),
        P(None, ("dp", "expert"), None),
        P(None, ("dp", "expert"), None),
        P(None, ("dp", "expert"), None),
        P(None, ("dp", "expert"), None),
        P(("dp", "expert"), None, None),
        P(("dp", "expert"), None, None),
        P(("dp", "expert"), None, None),
        P(("dp", "expert"), None, None),
        P(("dp", "expert"), None),
        P(("dp", "expert"), None),
        P(None, ("dp", "expert")),
        P(None, ("dp", "expert"), None),
        P(),
        P(),
        P("expert", None, "dp"),
        P("expert", "dp", None),
    )
    out_specs = P(None, ("dp", "expert"), None)
    return jax.shard_map(shards, mesh=mesh, in_specs=in_specs, out_specs=out_specs, check_vma=False)
```

profile of v0, /device:TPU:1, one launch (start us, length us, event | category | flops | bytes accessed | tf_op | source)
XLA Modules:
  0.0 609.5 jit_solution(8068935111660081858)
XLA Ops:
  6.5 2.0 collective-permute-start
  8.6 1.2 collective-permute-start.1
  10.6 4.9 gather_fusion.1
  15.5 5.0 gather_fusion.3
  20.9 84.7 %collective-permute-done = bf16[16,64,2048]{2,1,0:T(8,128)(2,1)} collective-permute-done((bf16[16,64,2048]{2,1,0:T(8,128)(2,1)}, bf16[16,64,2048]{2,1,0:T(8,128)(2,1)}, u32[]{:S(2)}, u32[]{:S(2)}) %collective-permute-start) | collective-permute-done | bytes 4194336 | tf_op jit(solution)/shard_map/ppermute | solution.py:14
  105.7 5.0 gather_fusion
  110.6 84.7 %collective-permute-done.1 = bf16[16,64,2048]{2,1,0:T(8,128)(2,1)} collective-permute-done((bf16[16,64,2048]{2,1,0:T(8,128)(2,1)}, bf16[16,64,2048]{2,1,0:T(8,128)(2,1)}, u32[]{:S(2)}, u32[]{:S(2)}) %collective-permute-start.1) | collective-permute-done | bytes 4194336 | tf_op jit(solution)/shard_map/ppermute | solution.py:14
  195.4 4.9 gather_fusion.2
  200.3 6.6 %select_select_fusion.3 = (bf16[16,64,2048]{2,1,0:T(8,128)(2,1)S(1)}, bf16[16,64,2048]{2,1,0:T(8,128)(2,1)S(1)}) fusion(bf16[16,64,2048]{2,1,0:T(8,128)(2,1)} %gather_fusion.1, bf16[16,64,2048]{2,1,0:T(8,128)(2,1)} %gather_fusion, pred[16]{0:T(512)(128)(4,1)S(1)} %get-tuple-element.49, pred[16]{0:T(512)(128)(4,1)S(1)} %get-tuple-element.51, ...), kind=kLoop, calls=%fused_computation.45 | loop fusion | flops 12582912 | bytes 25165872 | tf_op jit(solution)/shard_map/jit(_where)/select_n | solution.py:34
  207.8 1.3 copy-done.3
  209.1 4.4 copy.124
  214.5 4.4 copy.128
  220.1 3.6 fusion.135
  223.7 3.6 fusion.136
  227.3 5.3 gather_fusion.5
  232.6 5.4 gather_fusion.7
  238.0 5.7 copy.158
  243.7 1.4 copy.156
  245.5 2.5 fusion.14
  248.2 2.6 pad_maximum_fusion.5
  250.8 1.5 fusion.12
  254.4 57.3 %collective-permute-done.2 = bf16[16,65,2048]{2,0,1:T(8,128)(2,1)} collective-permute-done((bf16[16,65,2048]{2,0,1:T(8,128)(2,1)}, bf16[16,65,2048]{2,0,1:T(8,128)(2,1)}, u32[]{:S(2)}, u32[]{:S(2)}) %collective-permute-start.2) | collective-permute-done | bytes 4259872 | tf_op jit(solution)/shard_map/ppermute | solution.py:14
  311.7 17.2 %copy.125 = bf16[16,65,2048]{2,1,0:T(8,128)(2,1)} copy(bf16[16,65,2048]{2,0,1:T(8,128)(2,1)} %collective-permute-done.2) | data formatting | bytes 8519680 | tf_op jit(solution)/shard_map/ppermute | solution.py:14
  329.0 5.4 gather_fusion.4
  334.4 68.6 %collective-permute-done.3 = bf16[16,65,2048]{2,0,1:T(8,128)(2,1)} collective-permute-done((bf16[16,65,2048]{2,0,1:T(8,128)(2,1)}, bf16[16,65,2048]{2,0,1:T(8,128)(2,1)}, u32[]{:S(2)}, u32[]{:S(2)}) %collective-permute-start.3) | collective-permute-done | bytes 4259872 | tf_op jit(solution)/shard_map/ppermute | solution.py:14
  403.0 6.8 %copy.129 = bf16[16,65,2048]{2,1,0:T(8,128)(2,1)} copy(bf16[16,65,2048]{2,0,1:T(8,128)(2,1)} %collective-permute-done.3) | data formatting | bytes 8519680 | tf_op jit(solution)/shard_map/ppermute | solution.py:14
  409.7 5.3 gather_fusion.6
  415.1 11.1 %select_select_fusion.1 = (bf16[16,65,2048]{2,1,0:T(8,128)(2,1)}, bf16[16,65,2048]{2,1,0:T(8,128)(2,1)}) fusion(bf16[16,65,2048]{2,1,0:T(8,128)(2,1)} %gather_fusion.5, bf16[16,65,2048]{2,1,0:T(8,128)(2,1)} %gather_fusion.4, pred[16]{0:T(512)(128)(4,1)S(1)} %get-tuple-element.47, pred[16]{0:T(512)(128)(4,1)S(1)} %get-tuple-element.11, ...), kind=kLoop, calls=%fused_computation.31 | loop fusion | flops 12779520 | bytes 25559088 | tf_op jit(solution)/shard_map/jit(_where)/select_n | solution.py:34
  426.1 7.6 %reshape.798 = bf16[16,65,16,128]{3,2,1,0:T(8,128)(2,1)} reshape(bf16[16,65,2048]{2,1,0:T(8,128)(2,1)} %get-tuple-element.42) | data formatting | bytes 8519680 | tf_op jit(solution)/shard_map/concatenate | solution.py:156
  433.7 7.6 %reshape.795 = bf16[16,65,16,128]{3,2,1,0:T(8,128)(2,1)} reshape(bf16[16,65,2048]{2,1,0:T(8,128)(2,1)} %get-tuple-element.41) | data formatting | bytes 8519680 | tf_op jit(solution)/shard_map/concatenate | solution.py:153
  441.3 2.9 pad_maximum_fusion.2
  444.2 2.6 fusion.10
  447.0 2.9 pad_maximum_fusion.3
  449.9 3.4 fusion.8
  453.3 1.0 fusion.133
  455.5 10.8 %all_to_all.20 = bf16[16,4,2048]{2,1,0:T(4,128)(2,1)} all-to-all(bf16[16,4,2048]{2,1,0:T(4,128)(2,1)S(1)} %reshape.663), channel_id=1, replica_groups=mesh['dp'=8,'expert'=16] {'expert'}, dimensions={0} | all-to-all | bytes 524288 | tf_op jit(solution)/shard_map/all_to_all | solution.py:62
  467.5 10.8 %all_to_all.21 = bf16[16,4,2048]{2,1,0:T(4,128)(2,1)} all-to-all(bf16[16,4,2048]{2,1,0:T(4,128)(2,1)S(1)} %reshape.677), channel_id=1, replica_groups=mesh['dp'=8,'expert'=16] {'expert'}, dimensions={0} | all-to-all | bytes 524288 | tf_op jit(solution)/shard_map/all_to_all | solution.py:62
  478.6 11.8 %all-gather.5.cloned.1.call-done = bf16[128,4,2048]{2,1,0:T(4,128)(2,1)} async-done(((bf16[16,4,2048]{2,1,0:T(4,128)(2,1)}), bf16[128,4,2048]{2,1,0:T(4,128)(2,1)}) %all-gather.5.cloned.1.call-update) | async-done | bytes 2097168 | tf_op jit(solution)/shard_map/all_gather | solution.py:67
  490.4 11.3 %fusion.33 = bf16[128,1,4,2048]{3,0,2,1:T(8,128)(2,1)} fusion(bf16[1,1024,2048]{2,1,0:T(8,128)(2,1)} %param.37, bf16[1,2048,1024]{2,1,0:T(8,128)(2,1)} %param.36, bf16[128,4,2048]{2,1,0:T(4,128)(2,1)} %all-gather.5.cloned.1.call-done), kind=kOutput, calls=%fused_computation.49 | convolution fusion | flops 4297064448 | bytes 12582912 | tf_op jit(solution)/shard_map/secf,efd->secd/dot_general | solution.py:72
  501.8 15.8 %all-gather.7.cloned.1.call-done = bf16[128,4,2048]{2,1,0:T(4,128)(2,1)} async-done(((bf16[16,4,2048]{2,1,0:T(4,128)(2,1)}), bf16[128,4,2048]{2,1,0:T(4,128)(2,1)}) %all-gather.7.cloned.1.call-update) | async-done | bytes 2097168 | tf_op jit(solution)/shard_map/all_gather | solution.py:67
  517.6 11.4 %fusion.30 = bf16[128,1,4,2048]{3,0,2,1:T(8,128)(2,1)} fusion(bf16[1,1024,2048]{2,1,0:T(8,128)(2,1)} %param.37, bf16[1,2048,1024]{2,1,0:T(8,128)(2,1)} %param.36, bf16[128,4,2048]{2,1,0:T(4,128)(2,1)} %all-gather.7.cloned.1.call-done), kind=kOutput, calls=%fused_computation.48 | convolution fusion | flops 4297064448 | bytes 12582912 | tf_op jit(solution)/shard_map/secf,efd->secd/dot_general | solution.py:72
  529.9 20.6 %reduce-scatter.3.cloned.1.call-done = bf16[16,1,4,2048]{3,0,2,1:T(8,128)(2,1)} async-done(((bf16[128,1,4,2048]{3,0,2,1:T(8,128)(2,1)}), bf16[16,1,4,2048]{3,0,2,1:T(8,128)(2,1)}) %reduce-scatter.3.cloned.1.call-update) | async-done | bytes 262160 | tf_op jit(solution)/shard_map/reduce_scatter | solution.py:76
  550.5 1.9 copy.122
  552.4 6.8 %all-to-all-start.1 = ((bf16[16,4,2048]{2,1,0:T(4,128)(2,1)}), bf16[16,4,2048]{2,1,0:T(4,128)(2,1)S(1)}, u32[]{:S(2)}, u32[]{:S(2)}) async-start(bf16[16,4,2048]{2,1,0:T(4,128)(2,1)} %copy.122), calls=%async_computation.2 | async-start | bytes 524288 | tf_op jit(solution)/shard_map/all_to_all | solution.py:80
  559.5 26.0 %reduce-scatter.5.cloned.1.call-done = bf16[16,1,4,2048]{3,0,2,1:T(8,128)(2,1)} async-done(((bf16[128,1,4,2048]{3,0,2,1:T(8,128)(2,1)}), bf16[16,1,4,2048]{3,0,2,1:T(8,128)(2,1)}) %reduce-scatter.5.cloned.1.call-update) | async-done | bytes 262160 | tf_op jit(solution)/shard_map/reduce_scatter | solution.py:76
  585.5 1.9 copy.139
  587.4 6.6 %all-to-all-start.3 = ((bf16[16,4,2048]{2,1,0:T(4,128)(2,1)}), bf16[16,4,2048]{2,1,0:T(4,128)(2,1)S(1)}, u32[]{:S(2)}, u32[]{:S(2)}) async-start(bf16[16,4,2048]{2,1,0:T(4,128)(2,1)} %copy.139), calls=%async_computation.5 | async-start | bytes 524288 | tf_op jit(solution)/shard_map/all_to_all | solution.py:80
  594.3 7.2 %all-to-all-done.3 = bf16[16,4,2048]{2,1,0:T(4,128)(2,1)S(1)} async-done(((bf16[16,4,2048]{2,1,0:T(4,128)(2,1)}), bf16[16,4,2048]{2,1,0:T(4,128)(2,1)S(1)}, u32[]{:S(2)}, u32[]{:S(2)}) %all-to-all-start.3) | async-done | bytes 262176 | tf_op jit(solution)/shard_map/all_to_all | solution.py:80
  (132 shorter events, 12.0 us)
Async XLA Ops:
  6.5 522.9 %copy-start = (bf16[2048,16]{0,1:T(8,128)(2,1)S(1)}, bf16[2048,16]{0,1:T(8,128)(2,1)}, u32[]{:S(2)}) copy-start(bf16[2048,16]{0,1:T(8,128)(2,1)} %param.35) | copy-start | bytes 196612
  6.5 483.9 %all-gather.5.cloned.1.call-start = ((), (), s32[]{:S(2)}) async-start(), calls=%async_computation.8 | async-start | bytes 2359296 | tf_op jit(solution)/shard_map/all_gather | solution.py:67
  6.5 99.1 %collective-permute-start = (bf16[16,64,2048]{2,1,0:T(8,128)(2,1)}, bf16[16,64,2048]{2,1,0:T(8,128)(2,1)}, u32[]{:S(2)}, u32[]{:S(2)}) collective-permute-start(bf16[16,64,2048]{2,1,0:T(8,128)(2,1)} %param.26), channel_id=1, source_target_pairs={{0,1},{1,2},{2,3},{3,4},{4,5},{5,6},{6,7},{7,8},{8,9},{9,10},{10,1... | collective-permute-start | bytes 12582920 | tf_op jit(solution)/shard_map/ppermute | solution.py:14
  8.6 186.8 %collective-permute-start.1 = (bf16[16,64,2048]{2,1,0:T(8,128)(2,1)}, bf16[16,64,2048]{2,1,0:T(8,128)(2,1)}, u32[]{:S(2)}, u32[]{:S(2)}) collective-permute-start(bf16[16,64,2048]{2,1,0:T(8,128)(2,1)} %param.27), channel_id=1, source_target_pairs={{0,1},{1,2},{2,3},{3,4},{4,5},{5,6},{6,7},{7,8},{8,9},{9,10},{10,1... | collective-permute-start | bytes 12582920 | tf_op jit(solution)/shard_map/ppermute | solution.py:14
  15.5 5.1 copy-start.7
  15.5 5.2 copy-start.8
  15.5 5.3 copy-start.13
  15.5 5.4 copy-start.6
  15.5 5.4 copy-start.9
  206.9 2.2 copy-start.3
  206.9 6.6 %copy-start.5 = (bf16[16,64,2048]{2,1,0:T(8,128)(2,1)}, bf16[16,64,2048]{2,1,0:T(8,128)(2,1)S(1)}, u32[]{:S(2)}) copy-start(bf16[16,64,2048]{2,1,0:T(8,128)(2,1)S(1)} %get-tuple-element.44) | copy-start | bytes 12582916
  209.1 4.4 copy-start.1
  213.5 98.2 %collective-permute-start.2 = (bf16[16,65,2048]{2,0,1:T(8,128)(2,1)}, bf16[16,65,2048]{2,0,1:T(8,128)(2,1)}, u32[]{:S(2)}, u32[]{:S(2)}) collective-permute-start(bf16[16,65,2048]{2,0,1:T(8,128)(2,1)} %copy.124), channel_id=1, source_target_pairs={{0,1},{1,2},{2,3},{3,4},{4,5},{5,6},{6,7},{7,8},{8,9},{9,10},{10,1... | collective-permute-start | bytes 12779528 | tf_op jit(solution)/shard_map/ppermute | solution.py:14
  214.4 4.4 copy-start.2
  214.4 4.7 copy-start.10
  214.4 5.1 copy-start.12
  214.4 5.6 copy-start.17
  218.8 184.1 %collective-permute-start.3 = (bf16[16,65,2048]{2,0,1:T(8,128)(2,1)}, bf16[16,65,2048]{2,0,1:T(8,128)(2,1)}, u32[]{:S(2)}, u32[]{:S(2)}) collective-permute-start(bf16[16,65,2048]{2,0,1:T(8,128)(2,1)} %copy.128), channel_id=1, source_target_pairs={{0,1},{1,2},{2,3},{3,4},{4,5},{5,6},{6,7},{7,8},{8,9},{9,10},{10,1... | collective-permute-start | bytes 12779528 | tf_op jit(solution)/shard_map/ppermute | solution.py:14
  238.0 5.7 copy-start.4
  250.8 2.2 copy-start.14
  250.8 2.2 copy-start.18
  449.9 3.4 copy-start.15
  453.3 1.5 copy-start.11
  466.4 51.2 %all-gather.7.cloned.1.call-start = ((), (), s32[]{:S(2)}) async-start(), calls=%async_computation.9 | async-start | bytes 2359296 | tf_op jit(solution)/shard_map/all_gather | solution.py:67
  478.4 72.2 %reduce-scatter.3.cloned.1.call-start = ((), (), s32[]{:S(2)}) async-start(), calls=%async_computation.6 | async-start | bytes 2359296 | tf_op jit(solution)/shard_map/reduce_scatter | solution.py:76
  501.7 83.8 %reduce-scatter.5.cloned.1.call-start = ((), (), s32[]{:S(2)}) async-start(), calls=%async_computation.7 | async-start | bytes 2359296 | tf_op jit(solution)/shard_map/reduce_scatter | solution.py:76
  552.4 35.0 %all-to-all-start.1 = ((bf16[16,4,2048]{2,1,0:T(4,128)(2,1)}), bf16[16,4,2048]{2,1,0:T(4,128)(2,1)S(1)}, u32[]{:S(2)}, u32[]{:S(2)}) async-start(bf16[16,4,2048]{2,1,0:T(4,128)(2,1)} %copy.122), calls=%async_computation.2 | async-start | bytes 524288 | tf_op jit(solution)/shard_map/all_to_all | solution.py:80
  587.4 14.1 %all-to-all-start.3 = ((bf16[16,4,2048]{2,1,0:T(4,128)(2,1)}), bf16[16,4,2048]{2,1,0:T(4,128)(2,1)S(1)}, u32[]{:S(2)}, u32[]{:S(2)}) async-start(bf16[16,4,2048]{2,1,0:T(4,128)(2,1)} %copy.139), calls=%async_computation.5 | async-start | bytes 524288 | tf_op jit(solution)/shard_map/all_to_all | solution.py:80
  601.9 0.7 copy-start.16
Sparse Core Ops, SparseCore 0:
  466.5 23.8 all-gather.4
  492.1 25.4 all-gather.6
  520.0 30.4 reduce-scatter.2
  552.8 32.7 reduce-scatter.4
where the time goes:
time: 621 us; the launch traced here: 609 us
  waiting for transfers between devices  377 us (61%)
  local copies, waits for them, and re-layouts  105 us (17%)
  matrix products  43.5 us (7%)
  other arithmetic  31.1 us (5%)
  blocking collectives  21.6 us (3%)
  starting transfers between devices  17.1 us (3%)
  between operations  14.2 us (2%)
    ppermute x4, waiting for transfers between devices, passed_along(): return lax.ppermute(value, axis, pairs)  295 us
    reduce_scatter x2, waiting for transfers between devices, experts_apply(): lax.psum_scatter(partial_out, 'dp', scatter_dimension=0, tiled=True)  46.7 us
    all_gather x2, waiting for transfers between devices, experts_apply(): lax.all_gather(arrived, 'dp', axis=0, tiled=True)  27.6 us
    ppermute x2, local copies, waits for them, and re-layouts, passed_along(): return lax.ppermute(value, axis, pairs)  24 us
    dot_general x2, matrix products, experts_apply(): jnp.einsum('secf,efd->secd', units, w_out, preferred_element_type=jnp.flo...  22.7 us
    all_to_all x2, blocking collectives, experts_apply(): lax.all_to_all(outgoing, 'expert', split_axis=0, concat_axis=0, tiled=True)  21.6 us
    select_n x2, other arithmetic, reorder(): jnp.where(row_mask, far_keys, own_keys)  17.7 us
    all_to_all x2, starting transfers between devices, experts_apply(): lax.all_to_all(summed.reshape(expert_count, stack_size * capacity, width)...  13.3 us
  transfers between devices with their start and end apart: 10, of which 9 were waited for; matrix products, arithmetic and copies ran while one was open for 18% of the time, Pallas kernels for 0%

commit v1 on v0

v1 whole, which is shorter than its diff:
```python
import functools
import math

import jax
import jax.numpy as jnp
from jax import lax
from jax.experimental import pallas as pl
from jax.experimental.pallas import tpu as pltpu
from jax.sharding import PartitionSpec as P

epsilon = 1e-05
MESH = pl.DeviceIdType.MESH
BF = jnp.bfloat16
F32 = jnp.float32
LOW = -1e30
FLOOR = -1e20


def iota(shape, dim):
    return lax.broadcasted_iota(jnp.int32, shape, dim)


def as_column(row, n):
    return jnp.sum(jnp.where(iota((n, n), 0) == iota((n, n), 1), row, 0.0), axis=1, keepdims=True)


def pick(row, index_col, n):
    lanes = iota((n, n), 1).astype(F32)
    return jnp.sum(jnp.where(lanes == index_col, row, 0.0), axis=1, keepdims=True)


def inside(value, start, n):
    return (value >= start) & (value < start + n)


def remote_rank(row, start, n):
    far = jnp.where(inside(row, start, n), 0.0, 1.0)
    far_col = as_column(far, n)
    rank = jnp.sum(jnp.where(iota((n, n), 0) < iota((n, n), 1), far_col, 0.0), axis=0, keepdims=True)
    return far, rank


def bdot(a, b):
    return lax.dot_general(a, b, (((1,), (0,)), ((), ())), preferred_element_type=F32)


def tdot(a, b):
    return lax.dot_general(a, b, (((1,), (1,)), ((), ())), preferred_element_type=F32)


def attention_kernel(
    n_dp, n_ex, rows, cache, src, beams, chunks,
    hidden, q_self, k_new, v_new, q_cross, parents, key_scale, value_scale, gain,
    ck_hbm, cv_hbm, xk_hbm, xv_hbm,
    residual_ref, normed_ref,
    kbuf, vbuf, xkbuf, xvbuf, q_all, o_all, o_send, x_out, bias, bias_e, bias_x, scales,
    stat, par_own, par_in, q_d, q_e, in_c, in_d, in_e, o_d, o_e, back_c, back_d, back_e, stat_in, stat_in2,
    load_sem, send_sem, recv_sem,
):
    width = hidden.shape[2]
    heads = key_scale.shape[1]
    size = width // heads
    per_chunk = heads // chunks
    quarter = width // 4
    n_dev = n_dp * n_ex
    me = lax.axis_index("dp") * n_ex + lax.axis_index("expert")

    def at(offset):
        other = lax.rem(me + offset + n_dev, n_dev)
        return (other // n_ex, lax.rem(other, n_ex))

    barrier = pltpu.get_barrier_semaphore()
    for offset in (-1, -2, 1, 2):
        pl.semaphore_signal(barrier, inc=1, device_id=at(offset), device_id_type=MESH)

    loads = []
    for k, (source, buffer) in enumerate(
        ((ck_hbm, kbuf), (cv_hbm, vbuf), (xk_hbm, xkbuf), (xv_hbm, xvbuf))
    ):
        for c in range(chunks):
            loads.append((k, c, source, buffer))

    def load(k, c, source, buffer):
        part = width // chunks
        return pltpu.make_async_copy(
            source.at[:, pl.ds(pl.multiple_of(c * part, part), part)], buffer.at[c], load_sem.at[k, c]
        )

    for c in range(chunks):
        load(0, c, ck_hbm, kbuf).start()
        load(1, c, cv_hbm, vbuf).start()
    for c in range(chunks):
        load(2, c, xk_hbm, xkbuf).start()
        load(3, c, xv_hbm, xvbuf).start()

    par_own[...] = jnp.zeros_like(par_own)
    par_own[0:2, 0:rows] = parents[...]
    own = (me * rows).astype(F32)
    after = (lax.rem(me + 1, n_dev) * rows).astype(F32)
    after2 = (lax.rem(me + 2, n_dev) * rows).astype(F32)
    p0 = parents[0:1, :].astype(F32)
    p1 = parents[1:2, :].astype(F32)
    far0, rank0 = remote_rank(p0, own, rows)
    far1, rank1 = remote_rank(p1, own, rows)
    far0_col, rank0_col = as_column(far0, rows), as_column(rank0, rows)
    far1_col, rank1_col = as_column(far1, rows), as_column(rank1, rows)
    sub = iota((16, rows), 0)
    lane = iota((rows, 16), 1)

    def compact(value, far, rank):
        total = jnp.zeros((16, quarter), F32)
        for k in range(4):
            hot = ((sub >> 2) == k) & ((sub & 3).astype(F32) == rank) & (far > 0.5)
            total += bdot(jnp.where(hot, 1.0, 0.0).astype(BF), value[:, k * quarter:(k + 1) * quarter])
        return total.astype(BF)

    q_d[...] = compact(q_self[0], far0, rank0)
    q_e[...] = compact(q_self[1], far1, rank1)

    def remote(source, target, number, offset):
        return pltpu.make_async_remote_copy(
            src_ref=source, dst_ref=target, send_sem=send_sem.at[number], recv_sem=recv_sem.at[number],
            device_id=at(offset), device_id_type=MESH,
        )

    out_copies = [
        remote(par_own, par_in.at[0], 0, -1),
        remote(par_own, par_in.at[1], 1, -2),
        remote(q_d, in_d, 2, -1),
        remote(q_e, in_e, 3, -2),
        remote(q_self.at[1], in_c, 4, -1),
    ]
    pl.semaphore_wait(barrier, 4)
    for copy in out_copies:
        copy.start()

    sentence = (iota((2 * rows, 1), 0) & (rows - 1)) // beams
    ks = jnp.zeros((2 * rows, heads), F32)
    vs = jnp.zeros((2 * rows, heads), F32)
    for s in range(rows // beams):
        ks = jnp.where(sentence == s, key_scale[s:s + 1, :], ks)
        vs = jnp.where(sentence == s, value_scale[s:s + 1, :], vs)
    root = 1.0 / math.sqrt(size)
    scales[0, :, 0:heads] = ks * root
    scales[1, :, 0:heads] = vs
    n_cross = (rows // beams) * src
    bias_x[...] = jnp.where(
        iota((2 * rows, n_cross), 1) // src == (iota((2 * rows, n_cross), 0) & (rows - 1)) // beams, 0.0, LOW
    )
    q_all[0:rows, :] = q_self[0]
    q_all[rows:2 * rows, :] = q_self[1]

    for copy in out_copies:
        copy.wait()
    q_all[2 * rows:3 * rows, :] = in_c[...]
    a16, b16 = iota((16, 16), 0), iota((16, 16), 1)
    for k in range(4):
        take_d = jnp.where((b16 == a16 + 4 * k) & (a16 < 4), 1.0, 0.0).astype(BF)
        take_e = jnp.where((b16 == a16 - 4 + 4 * k) & (a16 >= 4) & (a16 < 8), 1.0, 0.0).astype(BF)
        q_all[3 * rows:4 * rows, k * quarter:(k + 1) * quarter] = (
            bdot(take_d, in_d[...]) + bdot(take_e, in_e[...])
        ).astype(BF)

    n0 = par_in[0, 0:1, 0:rows].astype(F32)
    n1 = par_in[0, 1:2, 0:rows].astype(F32)
    m1 = par_in[1, 1:2, 0:rows].astype(F32)
    p0_col, p1_col = as_column(p0, rows), as_column(p1, rows)
    n1_col = as_column(n1, rows)
    index = iota((rows, 1), 0).astype(F32)
    none = jnp.full((rows, 1), -1000.0, F32)

    def local(value):
        return jnp.where(inside(value, own, rows), value - own, -1.0)

    own_b = p1_col - own
    in_own = inside(p1_col, own, rows)
    row_b = jnp.where(in_own, local(pick(p0, own_b, rows)), -1.0)
    first_b = jnp.where(in_own, own_b, -1.0)
    in_next = inside(n1_col, after, rows)
    in_here = inside(n1_col, own, rows)
    row_c = jnp.where(
        in_next,
        local(pick(n0, n1_col - after, rows)),
        jnp.where(in_here, local(pick(p0, n1_col - own, rows)), -1.0),
    )
    first_c = jnp.where(in_here & jnp.logical_not(in_next), n1_col - own, -1.0)
    far_n, rank_n = remote_rank(n0, after, rows)
    far_m, rank_m = remote_rank(m1, after2, rows)
    i_col = iota((rows, rows), 0).astype(F32)
    val_d = jnp.sum(jnp.where((rank_n == i_col) & (far_n > 0.5), n0, 0.0), axis=1, keepdims=True)
    val_e = jnp.sum(jnp.where((rank_m == i_col - 4.0) & (far_m > 0.5), m1, 0.0), axis=1, keepdims=True)
    row_de = jnp.where(
        index < 4.0,
        local(val_d),
        jnp.where(
            (index < 8.0) & inside(val_e, after, rows), local(pick(n0, val_e - after, rows)), -1.0
        ),
    )
    row_sel = jnp.concatenate([local(p0_col), row_b, row_c, row_de], axis=0)
    first_sel = jnp.concatenate([index, first_b, first_c, none], axis=0)
    second_sel = jnp.concatenate([none, index, none, none], axis=0)
    slots = 4 * rows
    bias[...] = jnp.where((iota((slots, rows * cache), 1) // cache).astype(F32) == row_sel, 0.0, LOW)
    lane_e = iota((slots, 2 * rows), 1).astype(F32)
    bias_e[...] = jnp.where((lane_e == first_sel) | (lane_e - rows == second_sel), 0.0, LOW)

    stat[...] = jnp.zeros_like(stat)
    lanes = iota((slots, 128), 1)

    def self_chunk(c, carry):
        load(0, c, ck_hbm, kbuf).wait()
        load(1, c, cv_hbm, vbuf).wait()
        for j in range(per_chunk):
            h = c * per_chunk + j
            at_h = pl.ds(pl.multiple_of(h * size, size), size)
            q = q_all[:, at_h]
            k_extra = jnp.concatenate([k_new[0, :, at_h], k_new[1, :, at_h]], axis=0)
            v_extra = jnp.concatenate([v_new[0, :, at_h], v_new[1, :, at_h]], axis=0)
            s = tdot(q, kbuf[c, :, j * size:(j + 1) * size]) * root + bias[...]
            s_e = tdot(q, k_extra) * root + bias_e[...]
            top = jnp.maximum(
                jnp.maximum(jnp.max(s, axis=1, keepdims=True), jnp.max(s_e, axis=1, keepdims=True)), FLOOR
            )
            w = jnp.exp(s - top)
            w_e = jnp.exp(s_e - top)
            total = jnp.sum(w, axis=1, keepdims=True) + jnp.sum(w_e, axis=1, keepdims=True)
            o = bdot(w.astype(BF), vbuf[c, :, j * size:(j + 1) * size]) + bdot(w_e.astype(BF), v_extra)
            o_all[:, at_h] = o
            stat[0] = jnp.where(lanes == h, top, stat[0])
            stat[1] = jnp.where(lanes == h, total, stat[1])
        return carry

    lax.fori_loop(0, chunks, self_chunk, 0)

    o_send[...] = o_all[2 * rows:4 * rows, :].astype(BF)
    total_d = jnp.zeros((16, quarter), F32)
    total_e = jnp.zeros((16, quarter), F32)
    for k in range(4):
        piece = o_send[rows:2 * rows, k * quarter:(k + 1) * quarter]
        put_d = jnp.where(((a16 >> 2) == k) & (b16 == (a16 & 3)), 1.0, 0.0).astype(BF)
        put_e = jnp.where(((a16 >> 2) == k) & (b16 == (a16 & 3) + 4), 1.0, 0.0).astype(BF)
        total_d += bdot(put_d, piece)
        total_e += bdot(put_e, piece)
    o_d[...] = total_d.astype(BF)
    o_e[...] = total_e.astype(BF)
    back_copies = [
        remote(o_send.at[pl.ds(0, rows)], back_c, 5, 1),
        remote(o_d, back_d, 6, 1),
        remote(o_e, back_e, 7, 2),
        remote(stat.at[:, pl.ds(2 * rows, rows + 8)], stat_in, 8, 1),
        remote(stat.at[:, pl.ds(3 * rows, 8)], stat_in2, 9, 2),
    ]
    for copy in back_copies:
        copy.start()

    def cross_chunk(c, carry):
        load(2, c, xk_hbm, xkbuf).wait()
        load(3, c, xv_hbm, xvbuf).wait()
        for j in range(per_chunk):
            h = c * per_chunk + j
            at_h = pl.ds(pl.multiple_of(h * size, size), size)
            lanes_x = iota((2 * rows, 128), 1)
            ks_h = jnp.sum(jnp.where(lanes_x == h, scales[0], 0.0), axis=1, keepdims=True)
            vs_h = jnp.sum(jnp.where(lanes_x == h, scales[1], 0.0), axis=1, keepdims=True)
            q = jnp.concatenate([q_cross[0, :, at_h], q_cross[1, :, at_h]], axis=0)
            s = tdot(q, xkbuf[c, :, j * size:(j + 1) * size]) * ks_h + bias_x[...]
            top = jnp.max(s, axis=1, keepdims=True)
            w = jnp.exp(s - top)
            total = jnp.sum(w, axis=1, keepdims=True)
            o = bdot(w.astype(BF), xvbuf[c, :, j * size:(j + 1) * size])
            x_out[:, at_h] = o * (vs_h / total)
        return carry

    lax.fori_loop(0, chunks, cross_chunk, 0)

    for copy in back_copies:
        copy.wait()

    def spread(compact_ref, far_col, rank_col):
        pieces = []
        for k in range(4):
            hot = ((lane >> 2) == k) & ((lane & 3).astype(F32) == rank_col) & (far_col > 0.5)
            pieces.append(bdot(jnp.where(hot, 1.0, 0.0).astype(BF), compact_ref[...]))
        return pieces

    def spread_stat(ref, start, far_col, rank_col):
        top = jnp.where(far_col > 0.5, 0.0, FLOOR) + jnp.zeros((rows, 128), F32)
        total = jnp.zeros((rows, 128), F32)
        for j in range(4):
            hot = (rank_col == float(j)) & (far_col > 0.5)
            top += jnp.where(hot, ref[0, start + j:start + j + 1, :], 0.0)
            total += jnp.where(hot, ref[1, start + j:start + j + 1, :], 0.0)
        return top, total

    o_far0 = spread(back_d, far0_col, rank0_col)
    o_far1 = spread(back_e, far1_col, rank1_col)
    stats0 = [
        (stat[0, 0:rows, :], stat[1, 0:rows, :]),
        spread_stat(stat_in, rows, far0_col, rank0_col),
    ]
    stats1 = [
        (stat[0, rows:2 * rows, :], stat[1, rows:2 * rows, :]),
        (stat_in[0, 0:rows, :], stat_in[1, 0:rows, :]),
        spread_stat(stat_in2, 4, far1_col, rank1_col),
    ]

    def weights(stats):
        top = stats[0][0]
        for t, _ in stats[1:]:
            top = jnp.maximum(top, t)
        parts = [jnp.exp(t - top) for t, _ in stats]
        total = sum(w * l for w, (_, l) in zip(parts, stats))
        return [w / total for w in parts]

    w0 = weights(stats0)
    w1 = weights(stats1)
    per_quarter = heads // 4
    for t in range(2):
        for h in range(heads):
            at_h = slice(h * size, (h + 1) * size)
            k, j = h // per_quarter, h % per_quarter
            inner = slice(j * size, (j + 1) * size)
            if t == 0:
                mixed = o_all[0:rows, at_h] * w0[0][:, h:h + 1] + o_far0[k][:, inner] * w0[1][:, h:h + 1]
            else:
                mixed = (
                    o_all[rows:2 * rows, at_h] * w1[0][:, h:h + 1]
                    + back_c[:, at_h].astype(F32) * w1[1][:, h:h + 1]
                    + o_far1[k][:, inner] * w1[2][:, h:h + 1]
                )
            residual_ref[t, :, at_h] = (
                hidden[t, :, at_h].astype(F32) + mixed + x_out[t * rows:(t + 1) * rows, at_h]
            )
    for t in range(2):
        value = residual_ref[t]
        average = jnp.mean(value, axis=1, keepdims=True)
        centered = value - average
        variance = jnp.mean(centered * centered, axis=1, keepdims=True)
        normed_ref[t] = (centered * lax.rsqrt(variance + epsilon) * gain[...]).astype(BF)


def attention(hidden, q_self, k_new, v_new, q_cross, cache_keys, cache_values, cross_keys, cross_values,
              key_scale, value_scale, parents, norm_gain):
    steps, rows, width = hidden.shape
    heads = key_scale.shape[1]
    cache = cache_keys.shape[1]
    sentences, src = cross_keys.shape[:2]
    chunks = 4
    n_dp, n_ex = lax.axis_size("dp"), lax.axis_size("expert")
    part = width // chunks
    n_self, n_cross, slots = rows * cache, sentences * src, 4 * rows
    vmem = pl.BlockSpec(memory_space=pltpu.VMEM)
    hbm = pl.BlockSpec(memory_space=pl.ANY)
    quarter = width // 4
    return pl.pallas_call(
        functools.partial(attention_kernel, n_dp, n_ex, rows, cache, src, rows // sentences, chunks),
        out_shape=(
            jax.ShapeDtypeStruct((steps, rows, width), F32),
            jax.ShapeDtypeStruct((steps, rows, width), BF),
        ),
        in_specs=[vmem] * 9 + [hbm] * 4,
        out_specs=(vmem, vmem),
        scratch_shapes=[
            pltpu.VMEM((chunks, n_self, part), BF),
            pltpu.VMEM((chunks, n_self, part), BF),
            pltpu.VMEM((chunks, n_cross, part), BF),
            pltpu.VMEM((chunks, n_cross, part), BF),
            pltpu.VMEM((slots, width), BF),
            pltpu.VMEM((slots, width), F32),
            pltpu.VMEM((2 * rows, width), BF),
            pltpu.VMEM((2 * rows, width), F32),
            pltpu.VMEM((slots, n_self), F32),
            pltpu.VMEM((slots, 2 * rows), F32),
            pltpu.VMEM((2 * rows, n_cross), F32),
            pltpu.VMEM((2, 2 * rows, 128), F32),
            pltpu.VMEM((2, slots, 128), F32),
            pltpu.VMEM((8, 128), jnp.int32),
            pltpu.VMEM((2, 8, 128), jnp.int32),
            pltpu.VMEM((16, quarter), BF),
            pltpu.VMEM((16, quarter), BF),
            pltpu.VMEM((rows, width), BF),
            pltpu.VMEM((16, quarter), BF),
            pltpu.VMEM((16, quarter), BF),
            pltpu.VMEM((16, quarter), BF),
            pltpu.VMEM((16, quarter), BF),
            pltpu.VMEM((rows, width), BF),
            pltpu.VMEM((16, quarter), BF),
            pltpu.VMEM((16, quarter), BF),
            pltpu.VMEM((2, rows + 8, 128), F32),
            pltpu.VMEM((2, 8, 128), F32),
            pltpu.SemaphoreType.DMA((4, chunks)),
            pltpu.SemaphoreType.DMA((10,)),
            pltpu.SemaphoreType.DMA((10,)),
        ],
        compiler_params=pltpu.CompilerParams(
            collective_id=0, has_side_effects=True, vmem_limit_bytes=48 * 2**20
        ),
    )(
        hidden, q_self, k_new, v_new, q_cross, parents, key_scale, value_scale, norm_gain.reshape(1, width),
        cache_keys.reshape(n_self, width), cache_values.reshape(n_self, width),
        cross_keys.reshape(n_cross, width), cross_values.reshape(n_cross, width),
    )


def experts_apply(normed, chosen_ids, w_in, w_out):
    stack_size, row_count, top_count = chosen_ids.shape
    width = normed.shape[2]
    expert_count = lax.axis_size("expert") * w_in.shape[0]
    capacity = max(2, 2 * row_count * top_count // expert_count)
    picked_ids = chosen_ids.reshape(stack_size, row_count * top_count)
    one_hot = (
        picked_ids[:, :, None] == jnp.arange(expert_count, dtype=jnp.int32)[None, None, :]
    ).astype(jnp.int32)
    before = jnp.cumsum(one_hot, axis=1) - one_hot
    slot_pos = jnp.sum(before * one_hot, axis=2)
    column = (
        picked_ids * (stack_size * capacity)
        + jnp.arange(stack_size, dtype=jnp.int32)[:, None] * capacity
        + slot_pos
    )
    columns = expert_count * stack_size * capacity
    dispatch = (
        column.reshape(-1)[:, None] == jnp.arange(columns, dtype=jnp.int32)[None, :]
    ).astype(jnp.bfloat16)
    sources = jnp.repeat(normed.reshape(stack_size * row_count, width), top_count, axis=0)
    outgoing = jnp.einsum(
        "pc,pd->cd", dispatch, sources, preferred_element_type=jnp.float32
    ).astype(jnp.bfloat16)
    outgoing = outgoing.reshape(expert_count, stack_size * capacity, width)
    arrived = lax.all_to_all(outgoing, "expert", split_axis=0, concat_axis=0, tiled=True)
    arrived = arrived.reshape(lax.axis_size("expert"), w_in.shape[0], stack_size * capacity, width)
    units = jax.nn.relu(
        jnp.einsum(
            "secd,edf->secf",
            lax.all_gather(arrived, "dp", axis=0, tiled=True),
            w_in,
            preferred_element_type=jnp.float32,
        )
    ).astype(jnp.bfloat16)
    partial_out = jnp.einsum(
        "secf,efd->secd", units, w_out, preferred_element_type=jnp.float32
    ).astype(jnp.bfloat16)
    summed = (
        lax.psum_scatter(partial_out, "dp", scatter_dimension=0, tiled=True)
        .astype(jnp.float32)
        .astype(jnp.bfloat16)
    )
    returned = lax.all_to_all(
        summed.reshape(expert_count, stack_size * capacity, width),
        "expert",
        split_axis=0,
        concat_axis=0,
        tiled=True,
    )
    gathered = jnp.dot(
        dispatch, returned.reshape(columns, width), preferred_element_type=jnp.float32
    )
    return gathered.reshape(stack_size, row_count, top_count, width)


def finish(residual, normed, chosen_ids, router, w_in, w_out):
    expert_count = router.shape[1]
    logits = jnp.einsum("srd,de->sre", normed, router, preferred_element_type=jnp.float32)
    match_table = (
        chosen_ids[:, :, :, None] == jnp.arange(expert_count, dtype=jnp.int32)[None, None, None, :]
    )
    chosen = jnp.sum(jnp.where(match_table, logits[:, :, None, :], 0.0), axis=3)
    first_gate = jax.nn.sigmoid(chosen[:, :, 0] - chosen[:, :, 1])
    gate_mix = jnp.stack([first_gate, 1.0 - first_gate], axis=2)
    expert_out = experts_apply(normed, chosen_ids, w_in, w_out)
    return (residual + jnp.sum(gate_mix[:, :, :, None] * expert_out, axis=2)).astype(jnp.bfloat16)


def shards(
    hidden, q_self, k_new, v_new, q_cross, cache_keys, cache_values, cross_keys, cross_values,
    key_scale, value_scale, parents, expert_ids, norm_gain, router, w_in, w_out,
):
    residual, normed = attention(
        hidden, q_self, k_new, v_new, q_cross, cache_keys, cache_values, cross_keys, cross_values,
        key_scale, value_scale, parents, norm_gain,
    )
    return finish(residual, normed, expert_ids, router, w_in, w_out)


def solution(mesh):
    in_specs = (
        P(None, ("dp", "expert"), None),
        P(None, ("dp", "expert"), None),
        P(None, ("dp", "expert"), None),
        P(None, ("dp", "expert"), None),
        P(None, ("dp", "expert"), None),
        P(("dp", "expert"), None, None),
        P(("dp", "expert"), None, None),
        P(("dp", "expert"), None, None),
        P(("dp", "expert"), None, None),
        P(("dp", "expert"), None),
        P(("dp", "expert"), None),
        P(None, ("dp", "expert")),
        P(None, ("dp", "expert"), None),
        P(),
        P(),
        P("expert", None, "dp"),
        P("expert", "dp", None),
    )
    out_specs = P(None, ("dp", "expert"), None)
    return jax.shard_map(shards, mesh=mesh, in_specs=in_specs, out_specs=out_specs, check_vma=False)
```

time: 621 us -> 172 us (0.28)
  the two profiles are of different devices: /device:TPU:1 before, /device:TPU:0 now
where the time goes in v1:
time: 172 us
  waiting for transfers between devices  77.1 us (45%)
  Pallas kernels  29 us (17%)
  matrix products  17 us (10%)
  between operations  13.5 us (8%)
  blocking collectives  13.4 us (8%)
  local copies, waits for them, and re-layouts  13.3 us (8%)
  starting transfers between devices  7.02 us (4%)
    reduce_scatter x1, waiting for transfers between devices, experts_apply(): lax.psum_scatter(partial_out, 'dp', scatter_dimension=0, tiled=True)  37.9 us
    all_gather x1, waiting for transfers between devices, experts_apply(): lax.all_gather(arrived, 'dp', axis=0, tiled=True)  29.5 us
    pallas_call x1, Pallas kernels, attention(): pl.pallas_call(functools.partial(attention_kernel, n_dp, n_ex, rows, cach...  29 us
    dot_general x1, matrix products, experts_apply(): jnp.einsum('secf,efd->secd', units, w_out, preferred_element_type=jnp.flo...  16.2 us
    all_to_all x1, blocking collectives, experts_apply(): lax.all_to_all(outgoing, 'expert', split_axis=0, concat_axis=0, tiled=True)  13.4 us
    unnamed x25, local copies, waits for them, and re-layouts  10.2 us
    all_to_all x1, waiting for transfers between devices, experts_apply(): lax.all_to_all(summed.reshape(expert_count, stack_size * capacity, width)...  9.67 us
    all_to_all x1, starting transfers between devices, experts_apply(): lax.all_to_all(summed.reshape(expert_count, stack_size * capacity, width)...  6.98 us
  transfers between devices with their start and end apart: 3, of which 3 were waited for; matrix products, arithmetic and copies ran while one was open for 0% of the time, Pallas kernels for 0%

profile of v1, /device:TPU:0, one launch (start us, length us, event | category | flops | bytes accessed | tf_op | source)
XLA Modules:
  0.0 171.5 jit_solution(1868687814496471382)
XLA Ops:
  6.5 0.0 copy-start
  6.5 0.0 all-gather.3.cloned.1.call-start
  6.5 0.8 copy.33
  7.3 0.1 eq.66
  7.4 0.1 fusion.20
  7.5 0.1 reduce_window_sum.11
  7.6 0.2 select_reduce_fusion
  7.8 0.1 reduce_sum.34
  7.8 0.1 reduce_sum.33
  7.9 0.1 add.43
  8.0 0.1 add.44
  8.1 0.1 add_add_fusion
  8.2 0.1 mul.40
  8.3 0.0 copy-start.1
  8.3 2.2 %copy-done.1 = bf16[16,64,2048]{2,1,0:T(8,128)(2,1)S(1)} copy-done((bf16[16,64,2048]{2,1,0:T(8,128)(2,1)S(1)}, bf16[16,64,2048]{2,1,0:T(8,128)(2,1)}, u32[]{:S(2)}) %copy-start.1) | copy-done | bytes 4194328
  10.5 0.0 copy-start.2
  10.5 0.9 copy-done.2
  11.4 0.0 copy-start.3
  11.4 0.9 copy-done.3
  12.3 0.9 copy-done.4
  13.2 0.0 copy-start.5
  13.2 0.9 copy-done.5
  14.1 0.9 copy-done.6
  15.0 0.7 copy-done.7
  15.7 0.7 copy-done.8
  16.4 0.7 copy-done.9
  17.0 0.7 copy-done.10
  17.7 29.0 %shard_map.163 = (f32[2,16,2048]{2,1,0:T(8,128)S(1)}, bf16[2,16,2048]{2,1,0:T(8,128)(2,1)S(1)}) custom-call(bf16[2,16,2048]{2,1,0:T(8,128)(2,1)S(1)} %copy-done.2, bf16[2,16,2048]{2,1,0:T(8,128)(2,1)S(1)} %copy-done.3, bf16[2,16,2048]{2,1,0:T(8,128)(2,1)S(1)} %copy-done.4, bf16[2,16,2048]{2,1,0:T(8,128)(2,1)S(1)} %copy-done.5, ...), custom_call_target="tpu_custom_call" | custom-call | tf_op jit(solution)/shard_map/pallas_call | solution.py:355
  46.7 0.1 broadcast_in_dim.24
  46.8 0.1 reshape.112
  47.0 0.4 fusion.7
  47.4 13.4 %all_to_all.10 = bf16[16,8,2048]{2,1,0:T(8,128)(2,1)} all-to-all(bf16[16,8,2048]{2,1,0:T(8,128)(2,1)S(1)} %fusion.7), channel_id=1, replica_groups=mesh['dp'=8,'expert'=16] {'expert'}, dimensions={0} | all-to-all | bytes 1048576 | tf_op jit(solution)/shard_map/all_to_all | solution.py:430
  60.8 0.0 all-gather.3.cloned.1.call-update
  60.8 0.0 reduce-scatter.2.cloned.1.call-start
  60.9 29.5 %all-gather.3.cloned.1.call-done = bf16[128,8,2048]{2,1,0:T(8,128)(2,1)} async-done(((bf16[16,8,2048]{2,1,0:T(8,128)(2,1)}), bf16[128,8,2048]{2,1,0:T(8,128)(2,1)}) %all-gather.3.cloned.1.call-update) | async-done | bytes 4194320 | tf_op jit(solution)/shard_map/all_gather | solution.py:435
  90.4 16.2 %convert_bitcast_fusion = bf16[128,1,8,2048]{3,0,2,1:T(8,128)(2,1)} fusion(bf16[1,1024,2048]{2,1,0:T(8,128)(2,1)} %param.33, bf16[1,2048,1024]{2,1,0:T(8,128)(2,1)} %param.32, bf16[128,8,2048]{2,1,0:T(8,128)(2,1)} %all-gather.3.cloned.1.call-done), kind=kOutput, calls=%fused_computation.5 | convolution fusion | flops 8594128896 | bytes 16777216 | tf_op jit(solution)/shard_map/secf,efd->secd/dot_general | solution.py:440
  106.5 0.0 reduce-scatter.2.cloned.1.call-update
  106.5 37.9 %reduce-scatter.2.cloned.1.call-done = bf16[16,1,8,2048]{3,0,2,1:T(8,128)(2,1)} async-done(((bf16[128,1,8,2048]{3,0,2,1:T(8,128)(2,1)}), bf16[16,1,8,2048]{3,0,2,1:T(8,128)(2,1)}) %reduce-scatter.2.cloned.1.call-update) | async-done | bytes 524304 | tf_op jit(solution)/shard_map/reduce_scatter | solution.py:444
  144.4 2.1 %copy.37 = bf16[16,8,2048]{2,1,0:T(8,128)(2,1)} copy(bf16[16,8,2048]{2,0,1:T(8,128)(2,1)} %bitcast.50) | data formatting | bytes 1048576 | tf_op jit(solution)/shard_map/reshape | solution.py:449
  146.6 7.0 %all-to-all-start.1 = ((bf16[16,8,2048]{2,1,0:T(8,128)(2,1)}), bf16[16,8,2048]{2,1,0:T(8,128)(2,1)S(1)}, u32[]{:S(2)}, u32[]{:S(2)}) async-start(bf16[16,8,2048]{2,1,0:T(8,128)(2,1)} %copy.37), calls=%async_computation.2 | async-start | bytes 1048576 | tf_op jit(solution)/shard_map/all_to_all | solution.py:448
  153.6 0.0 copy-done
  153.6 0.1 fusion.18
  153.7 0.1 copy.35
  153.8 0.0 copy-done.11
  153.8 0.2 select_reduce_fusion.1
  154.0 9.7 %all-to-all-done.1 = bf16[16,8,2048]{2,1,0:T(8,128)(2,1)S(1)} async-done(((bf16[16,8,2048]{2,1,0:T(8,128)(2,1)}), bf16[16,8,2048]{2,1,0:T(8,128)(2,1)S(1)}, u32[]{:S(2)}, u32[]{:S(2)}) %all-to-all-start.1) | async-done | bytes 524320 | tf_op jit(solution)/shard_map/all_to_all | solution.py:448
  163.7 0.3 fusion.12
  164.0 0.7 add_convert_fusion
  (11 shorter events, 0.0 us)
Async XLA Ops:
  6.5 147.0 %copy-start = (bf16[2048,16]{0,1:T(8,128)(2,1)S(1)}, bf16[2048,16]{0,1:T(8,128)(2,1)}, u32[]{:S(2)}) copy-start(bf16[2048,16]{0,1:T(8,128)(2,1)} %param.31) | copy-start | bytes 196612
  6.5 83.8 %all-gather.3.cloned.1.call-start = ((), (), s32[]{:S(2)}) async-start(), calls=%async_computation.4 | async-start | bytes 4718592 | tf_op jit(solution)/shard_map/all_gather | solution.py:435
  8.3 2.2 %copy-start.1 = (bf16[16,64,2048]{2,1,0:T(8,128)(2,1)S(1)}, bf16[16,64,2048]{2,1,0:T(8,128)(2,1)}, u32[]{:S(2)}) copy-start(bf16[16,64,2048]{2,1,0:T(8,128)(2,1)} %param.22) | copy-start | bytes 12582916
  10.5 0.9 copy-start.2
  11.4 0.9 copy-start.3
  12.3 0.9 copy-start.4
  13.2 0.9 copy-start.5
  14.1 0.9 copy-start.6
  15.0 0.7 copy-start.7
  15.7 0.7 copy-start.8
  16.4 0.7 copy-start.9
  17.0 0.7 copy-start.10
  60.8 83.6 %reduce-scatter.2.cloned.1.call-start = ((), (), s32[]{:S(2)}) async-start(), calls=%async_computation.3 | async-start | bytes 4718592 | tf_op jit(solution)/shard_map/reduce_scatter | solution.py:444
  106.5 47.3 %copy-start.11 = (s32[2,16,2]{1,2,0:T(2,128)S(1)}, s32[2,16,2]{1,2,0:T(2,128)}, u32[]{:S(2)}) copy-start(s32[2,16,2]{1,2,0:T(2,128)} %param.29) | copy-start | bytes 772
  146.6 17.1 %all-to-all-start.1 = ((bf16[16,8,2048]{2,1,0:T(8,128)(2,1)}), bf16[16,8,2048]{2,1,0:T(8,128)(2,1)S(1)}, u32[]{:S(2)}, u32[]{:S(2)}) async-start(bf16[16,8,2048]{2,1,0:T(8,128)(2,1)} %copy.37), calls=%async_computation.2 | async-start | bytes 1048576 | tf_op jit(solution)/shard_map/all_to_all | solution.py:448
Sparse Core Ops, SparseCore 0:
  60.9 29.3 all-gather.2
  106.7 37.7 reduce-scatter.1

commit v2 on v1

--- a/solution.py
+++ b/solution.py
@@ -50,12 +50,13 @@
 
 def attention_kernel(
     n_dp, n_ex, rows, cache, src, beams, chunks,
-    hidden, q_self, k_new, v_new, q_cross, parents, key_scale, value_scale, gain,
+    hidden_hbm, q_self_hbm, k_new_hbm, v_new_hbm, q_cross_hbm, parents_hbm, ks_hbm, vs_hbm, gain_hbm,
     ck_hbm, cv_hbm, xk_hbm, xv_hbm,
     residual_ref, normed_ref,
+    hidden, q_self, k_new, v_new, q_cross, parents, key_scale, value_scale, gain,
     kbuf, vbuf, xkbuf, xvbuf, q_all, o_all, o_send, x_out, bias, bias_e, bias_x, scales,
     stat, par_own, par_in, q_d, q_e, in_c, in_d, in_e, o_d, o_e, back_c, back_d, back_e, stat_in, stat_in2,
-    load_sem, send_sem, recv_sem,
+    load_sem, small_sem, send_sem, recv_sem,
 ):
     width = hidden.shape[2]
     heads = key_scale.shape[1]
@@ -73,19 +74,22 @@
     for offset in (-1, -2, 1, 2):
         pl.semaphore_signal(barrier, inc=1, device_id=at(offset), device_id_type=MESH)
 
-    loads = []
-    for k, (source, buffer) in enumerate(
-        ((ck_hbm, kbuf), (cv_hbm, vbuf), (xk_hbm, xkbuf), (xv_hbm, xvbuf))
-    ):
-        for c in range(chunks):
-            loads.append((k, c, source, buffer))
-
     def load(k, c, source, buffer):
         part = width // chunks
         return pltpu.make_async_copy(
             source.at[:, pl.ds(pl.multiple_of(c * part, part), part)], buffer.at[c], load_sem.at[k, c]
         )
 
+    small = [
+        pltpu.make_async_copy(source, target, small_sem.at[i])
+        for i, (source, target) in enumerate((
+            (parents_hbm, parents), (q_self_hbm, q_self), (k_new_hbm, k_new), (v_new_hbm, v_new),
+            (ks_hbm, key_scale), (vs_hbm, value_scale), (q_cross_hbm, q_cross), (hidden_hbm, hidden),
+            (gain_hbm, gain),
+        ))
+    ]
+    for copy in small:
+        copy.start()
     for c in range(chunks):
         load(0, c, ck_hbm, kbuf).start()
         load(1, c, cv_hbm, vbuf).start()
@@ -94,6 +98,8 @@
         load(3, c, xv_hbm, xvbuf).start()
 
     par_own[...] = jnp.zeros_like(par_own)
+    small[0].wait()
+    small[1].wait()
     par_own[0:2, 0:rows] = parents[...]
     own = (me * rows).astype(F32)
     after = (lax.rem(me + 1, n_dev) * rows).astype(F32)
@@ -134,6 +140,8 @@
     for copy in out_copies:
         copy.start()
 
+    small[4].wait()
+    small[5].wait()
     sentence = (iota((2 * rows, 1), 0) & (rows - 1)) // beams
     ks = jnp.zeros((2 * rows, heads), F32)
     vs = jnp.zeros((2 * rows, heads), F32)
@@ -150,6 +158,8 @@
     q_all[0:rows, :] = q_self[0]
     q_all[rows:2 * rows, :] = q_self[1]
 
+    for i in (2, 3, 6, 7, 8):
+        small[i].wait()
     for copy in out_copies:
         copy.wait()
     q_all[2 * rows:3 * rows, :] = in_c[...]
@@ -358,9 +368,13 @@
             jax.ShapeDtypeStruct((steps, rows, width), F32),
             jax.ShapeDtypeStruct((steps, rows, width), BF),
         ),
-        in_specs=[vmem] * 9 + [hbm] * 4,
+        in_specs=[hbm] * 13,
         out_specs=(vmem, vmem),
-        scratch_shapes=[
+        scratch_shapes=[pltpu.VMEM((steps, rows, width), BF)] * 5 + [
+            pltpu.VMEM((steps, rows), jnp.int32),
+            pltpu.VMEM((sentences, heads), F32),
+            pltpu.VMEM((sentences, heads), F32),
+            pltpu.VMEM((1, width), F32),
             pltpu.VMEM((chunks, n_self, part), BF),
             pltpu.VMEM((chunks, n_self, part), BF),
             pltpu.VMEM((chunks, n_cross, part), BF),
@@ -389,11 +403,12 @@
             pltpu.VMEM((2, rows + 8, 128), F32),
             pltpu.VMEM((2, 8, 128), F32),
             pltpu.SemaphoreType.DMA((4, chunks)),
+            pltpu.SemaphoreType.DMA((9,)),
             pltpu.SemaphoreType.DMA((10,)),
             pltpu.SemaphoreType.DMA((10,)),
         ],
         compiler_params=pltpu.CompilerParams(
-            collective_id=0, has_side_effects=True, vmem_limit_bytes=48 * 2**20
+            collective_id=0, has_side_effects=True, vmem_limit_bytes=60 * 2**20
         ),
     )(
         hidden, q_self, k_new, v_new, q_cross, parents, key_scale, value_scale, norm_gain.reshape(1, width),
@@ -402,73 +417,325 @@
     )
 
 
-def experts_apply(normed, chosen_ids, w_in, w_out):
-    stack_size, row_count, top_count = chosen_ids.shape
-    width = normed.shape[2]
-    expert_count = lax.axis_size("expert") * w_in.shape[0]
-    capacity = max(2, 2 * row_count * top_count // expert_count)
-    picked_ids = chosen_ids.reshape(stack_size, row_count * top_count)
-    one_hot = (
-        picked_ids[:, :, None] == jnp.arange(expert_count, dtype=jnp.int32)[None, None, :]
-    ).astype(jnp.int32)
-    before = jnp.cumsum(one_hot, axis=1) - one_hot
-    slot_pos = jnp.sum(before * one_hot, axis=2)
-    column = (
-        picked_ids * (stack_size * capacity)
-        + jnp.arange(stack_size, dtype=jnp.int32)[:, None] * capacity
-        + slot_pos
+def experts_kernel(
+    n_dp, n_ex, cap,
+    residual_hbm, normed_hbm, ids_hbm, router_hbm, w_in_hbm, w_out_hbm,
+    out_ref,
+    residual, normed, ids, ids_all, router, w_in, w_out, outgoing, xbuf, units, p_mine, p_send, p_back,
+    rs_a, rs_b, fin_a, fin_b, home, returned, y_send, y_back,
+    load_sem, pair_s, pair_r, a2a_s, a2a_r, near_s, near_r, fwd_s, fwd_r, sib_s, sib_r, part_s, part_r,
+    rs_s, rs_r, fin_s, fin_r, ret_s, ret_r,
+):
+    steps, rows = ids.shape[0], ids.shape[2]
+    tokens = steps * rows
+    width = residual.shape[1]
+    half = width // 2
+    hidden_units = w_in.shape[1]
+    slots = 2 * steps * cap
+    chunk = n_ex * slots
+    group = chunk // 4
+    dp = lax.axis_index("dp")
+    me = lax.axis_index("expert")
+    core = lax.rem(dp, 2)
+    n_y = n_dp // 2
+    place = dp // 2
+    sibling = (dp + 1 - 2 * core, me)
+    up_y = (lax.rem(place + 1, n_y) * 2 + core, me)
+    down_y = (lax.rem(place + n_y - 1, n_y) * 2 + core, me)
+
+    def peer(o):
+        return (dp, lax.rem(me + o, n_ex))
+
+    def peer_back(o):
+        return (dp, lax.rem(me - o + n_ex, n_ex))
+
+    barrier = pltpu.get_barrier_semaphore()
+    others = [sibling, up_y, down_y] + [peer(o) for o in range(1, n_ex)]
+    for other in others:
+        pl.semaphore_signal(barrier, inc=1, device_id=other, device_id_type=MESH)
+
+    mine = pl.ds(pl.multiple_of(core * tokens, tokens), tokens)
+    theirs = pl.ds(pl.multiple_of((1 - core) * tokens, tokens), tokens)
+    loads = [
+        pltpu.make_async_copy(normed_hbm, normed.at[mine], load_sem.at[0]),
+        pltpu.make_async_copy(ids_hbm, ids, load_sem.at[1]),
+        pltpu.make_async_copy(router_hbm, router, load_sem.at[2]),
+        pltpu.make_async_copy(w_in_hbm, w_in, load_sem.at[3]),
+        pltpu.make_async_copy(w_out_hbm, w_out, load_sem.at[4]),
+        pltpu.make_async_copy(residual_hbm, residual, load_sem.at[5]),
+    ]
+    for copy in loads:
+        copy.start()
+
+    started = []
+
+    def send(source, target, s_sem, r_sem, device):
+        copy = pltpu.make_async_remote_copy(
+            src_ref=source, dst_ref=target, send_sem=s_sem, recv_sem=r_sem,
+            device_id=device, device_id_type=MESH,
+        )
+        copy.start()
+        started.append(copy)
+        return copy
+
+    loads[0].wait()
+    loads[1].wait()
+    for t in range(steps):
+        named = [as_column(ids[t, k:k + 1, :].astype(F32), rows).astype(jnp.int32) for k in range(2)]
+        ids_all[core, t * rows:(t + 1) * rows, :] = jnp.where(iota((rows, 128), 1) == 0, named[0], named[1])
+    pl.semaphore_wait(barrier, len(others))
+    pair = [
+        send(normed.at[mine], normed.at[mine], pair_s.at[0], pair_r.at[0], sibling),
+        send(ids_all.at[core], ids_all.at[core], pair_s.at[1], pair_r.at[1], sibling),
+    ]
+    for copy in pair:
+        copy.wait_recv()
+
+    lane_x = iota((tokens, 128), 1)
+    lower = (iota((tokens, tokens), 1) < iota((tokens, tokens), 0)) & (
+        iota((tokens, tokens), 0) // rows == iota((tokens, tokens), 1) // rows
     )
-    columns = expert_count * stack_size * capacity
-    dispatch = (
-        column.reshape(-1)[:, None] == jnp.arange(columns, dtype=jnp.int32)[None, :]
-    ).astype(jnp.bfloat16)
-    sources = jnp.repeat(normed.reshape(stack_size * row_count, width), top_count, axis=0)
-    outgoing = jnp.einsum(
-        "pc,pd->cd", dispatch, sources, preferred_element_type=jnp.float32
-    ).astype(jnp.bfloat16)
-    outgoing = outgoing.reshape(expert_count, stack_size * capacity, width)
-    arrived = lax.all_to_all(outgoing, "expert", split_axis=0, concat_axis=0, tiled=True)
-    arrived = arrived.reshape(lax.axis_size("expert"), w_in.shape[0], stack_size * capacity, width)
-    units = jax.nn.relu(
-        jnp.einsum(
-            "secd,edf->secf",
-            lax.all_gather(arrived, "dp", axis=0, tiled=True),
-            w_in,
-            preferred_element_type=jnp.float32,
+    lower = jnp.where(lower, 1.0, 0.0).astype(BF)
+    step_of = (iota((tokens, 1), 0) // rows)
+    hots = []
+    for c in range(2):
+        named = [ids_all[c, :, k:k + 1] for k in range(2)]
+        one_hot = [lane_x == n for n in named]
+        count = jnp.where(one_hot[0] | one_hot[1], 1.0, 0.0).astype(BF)
+        before = bdot(lower, count)
+        pair_hot = []
+        for k in range(2):
+            spot = jnp.sum(jnp.where(one_hot[k], before, 0.0), axis=1, keepdims=True).astype(jnp.int32)
+            distance = named[k] - me
+            distance = jnp.where(distance < 0, distance + n_ex, distance)
+            column = distance * slots + (c * steps * cap + spot) + step_of * cap
+            pair_hot.append(iota((tokens, chunk), 1) == column)
+        hots.append(pair_hot)
+    dispatch = jnp.concatenate([jnp.where(h[0] | h[1], 1.0, 0.0).astype(BF) for h in hots], axis=0)
+    at_half = pl.ds(pl.multiple_of(core * half, half), half)
+    outgoing[...] = lax.dot_general(
+        dispatch, normed[:, at_half], (((0,), (0,)), ((), ())), preferred_element_type=F32
+    ).astype(BF)
+
+    def block(o):
+        return pl.ds(o * slots, slots)
+
+    arrivals = [None]
+    for o in range(1, n_ex):
+        arrivals.append(
+            send(outgoing.at[block(o)], xbuf.at[core, 0, block(o)], a2a_s.at[o], a2a_r.at[o], peer(o))
         )
-    ).astype(jnp.bfloat16)
-    partial_out = jnp.einsum(
-        "secf,efd->secd", units, w_out, preferred_element_type=jnp.float32
-    ).astype(jnp.bfloat16)
-    summed = (
-        lax.psum_scatter(partial_out, "dp", scatter_dimension=0, tiled=True)
-        .astype(jnp.float32)
-        .astype(jnp.bfloat16)
+    xbuf[core, 0, block(0), :] = outgoing[block(0), :]
+
+    loads[2].wait()
+    logits = tdot(normed[...], router[...])
+    lane_e = iota((tokens, n_ex), 1)
+    gates = []
+    for c in range(2):
+        part = logits[c * tokens:(c + 1) * tokens]
+        picked = [
+            jnp.sum(jnp.where(lane_e == ids_all[c, :, k:k + 1], part, 0.0), axis=1, keepdims=True)
+            for k in range(2)
+        ]
+        first = 1.0 / (1.0 + jnp.exp(picked[1] - picked[0]))
+        gates.append(
+            jnp.where(hots[c][0], first, 0.0) + jnp.where(hots[c][1], 1.0 - first, 0.0)
+        )
+
+    def piece(g):
+        return pl.ds(g * group, group)
+
+    per_group = n_ex // 4
+
+    def to_sibling(k, g):
+        return send(
+            xbuf.at[core, k, piece(g)], xbuf.at[core, k, piece(g)], sib_s.at[k, g], sib_r.at[k, g], sibling
+        )
+
+    tile = min(256, half, hidden_units)
+
+    def compute(k):
+        def first(j, carry):
+            cols = pl.ds(pl.multiple_of(j * tile, tile), tile)
+            a = bdot(xbuf[0, k], w_in[0:half, cols]) + bdot(xbuf[1, k], w_in[half:width, cols])
+            units[:, cols] = jnp.maximum(a, 0.0).astype(BF)
+            return carry
+
+        lax.fori_loop(0, hidden_units // tile, first, 0)
+
+        def second(base, target):
+            def step(j, carry):
+                cols = pl.ds(pl.multiple_of(base + j * tile, tile), tile)
+                target[k, :, pl.ds(pl.multiple_of(j * tile, tile), tile)] = bdot(
+                    units[...], w_out[:, cols]
+                ).astype(BF)
+                return carry
+
+            lax.fori_loop(0, half // tile, step, 0)
+
+        second((1 - core) * half, p_send)
+        copy = send(p_send.at[k], p_back.at[k], part_s.at[k], part_r.at[k], sibling)
+        second(core * half, p_mine)
+        return copy
+
+    def reduce_part(k, g):
+        return p_mine[k, piece(g), :].astype(F32) + p_back[k, piece(g), :].astype(F32)
+
+    sib = {}
+    near = {}
+    for g in range(4):
+        for o in range(g * per_group, (g + 1) * per_group):
+            if o:
+                arrivals[o].wait_recv()
+        near[1, g] = send(xbuf.at[core, 0, piece(g)], xbuf.at[core, 1, piece(g)], near_s.at[0, g], near_r.at[0, g], up_y)
+        near[2, g] = send(xbuf.at[core, 0, piece(g)], xbuf.at[core, 2, piece(g)], near_s.at[1, g], near_r.at[1, g], down_y)
+        sib[0, g] = to_sibling(0, g)
+    loads[3].wait()
+    loads[4].wait()
+    for g in range(4):
+        sib[0, g].wait_recv()
+    parts = [compute(0)]
+    far = []
+    for g in range(4):
+        for k in (1, 2):
+            near[k, g].wait_recv()
+            if (k == 1) == (g < 2):
+                far.append(send(
+                    xbuf.at[core, k, piece(g)], xbuf.at[core, 3, piece(g)], fwd_s.at[g], fwd_r.at[g],
+                    up_y if k == 1 else down_y,
+                ))
+            sib[k, g] = to_sibling(k, g)
+    for k in (1, 2):
+        for g in range(4):
+            sib[k, g].wait_recv()
+        parts.append(compute(k))
+    for g in range(4):
+        far[g].wait_recv()
+        sib[3, g] = to_sibling(3, g)
+
+    final = {}
+
+    def finish_near(k, g, extra=None):
+        value = reduce_part(k, g)
+        if extra is not None:
+            value += extra.astype(F32)
+        p_send[k, piece(g), :] = value.astype(BF)
+        final[k, g] = send(
+            p_send.at[k, piece(g)], (fin_b if k == 1 else fin_a).at[piece(g)],
+            fin_s.at[k - 1, g], fin_r.at[k - 1, g], down_y if k == 1 else up_y,
+        )
+
+    parts[0].wait()
+    parts[1].wait()
+    parts[2].wait()
+    for g in range(4):
+        finish_near(1 if g < 2 else 2, g)
+    home[...] = p_mine[0].astype(F32) + p_back[0].astype(F32)
+    for g in range(4):
+        sib[3, g].wait_recv()
+    parts.append(compute(3))
+    parts[3].wait()
+    relay = []
+    for g in range(4):
+        p_send[3, piece(g), :] = reduce_part(3, g).astype(BF)
+        relay.append(send(
+            p_send.at[3, piece(g)], (rs_a if g < 2 else rs_b).at[pl.ds((g % 2) * group, group)],
+            rs_s.at[g], rs_r.at[g], up_y if g < 2 else down_y,
+        ))
+    for g in (0, 2, 1, 3):
+        relay[g].wait_recv()
+        source = rs_a if g < 2 else rs_b
+        finish_near(2 if g < 2 else 1, g, source[pl.ds((g % 2) * group, group), :])
+    replies = [None] * n_ex
+    for g in (2, 3, 0, 1):
+        final[1, g].wait_recv()
+        final[2, g].wait_recv()
+        total = home[piece(g), :] + fin_a[piece(g), :].astype(F32) + fin_b[piece(g), :].astype(F32)
+        outgoing_rows = total.astype(BF)
+        p_mine[0, piece(g), :] = outgoing_rows
+        for o in range(g * per_group, (g + 1) * per_group):
+            if o:
+                replies[o] = send(
+                    p_mine.at[0, block(o)], returned.at[block(o)], ret_s.at[o], ret_r.at[o], peer_back(o)
+                )
+    returned[block(0), :] = p_mine[0, block(0), :]
+    for o in range(1, n_ex):
+        replies[o].wait_recv()
+    mix = []
+    for c in range(2):
+        high = gates[c].astype(BF)
+        low = (gates[c] - high.astype(F32)).astype(BF)
+        mix.append((high, low))
+
+    back = returned[...]
+    ys = [bdot(high, back) + bdot(low, back) for high, low in mix]
+    is_first = core == 0
+    y_send[...] = jnp.where(is_first, ys[1], ys[0])
+    swap = send(y_send, y_back, pair_s.at[2], pair_r.at[2], sibling)
+    own_y = jnp.where(is_first, ys[0], ys[1])
+    loads[5].wait()
+    residual[:, at_half] = residual[:, at_half] + own_y
+    swap.wait_recv()
+    at_other = pl.ds(pl.multiple_of((1 - core) * half, half), half)
+    residual[:, at_other] = residual[:, at_other] + y_back[...]
+    for t in range(steps):
+        out_ref[t] = residual[t * rows:(t + 1) * rows, :].astype(BF)
+    parts_done = {id(p) for p in parts}
+    for copy in started:
+        if id(copy) not in parts_done:
+            copy.wait_send()
+
+
+def experts(residual, normed, expert_ids, router, w_in, w_out):
+    steps, rows, width = residual.shape
+    n_dp, n_ex = lax.axis_size("dp"), lax.axis_size("expert")
+    tokens = steps * rows
+    hidden_units = w_in.shape[2]
+    half = width // 2
+    cap = 4 * rows // n_ex
+    slots = 2 * steps * cap
+    chunk = n_ex * slots
+    vmem = pl.BlockSpec(memory_space=pltpu.VMEM)
+    hbm = pl.BlockSpec(memory_space=pl.ANY)
+    dma = pltpu.SemaphoreType.DMA
+    return pl.pallas_call(
+        functools.partial(experts_kernel, n_dp, n_ex, cap),
+        out_shape=jax.ShapeDtypeStruct((steps, rows, width), BF),
+        in_specs=[hbm] * 6,
+        out_specs=vmem,
+        scratch_shapes=[
+            pltpu.VMEM((tokens, width), F32),
+            pltpu.VMEM((2 * tokens, width), BF),
+            pltpu.VMEM((steps, 2, rows), jnp.int32),
+            pltpu.VMEM((2, tokens, 128), jnp.int32),
+            pltpu.VMEM((n_ex, width), BF),
+            pltpu.VMEM((width, hidden_units), BF),
+            pltpu.VMEM((hidden_units, width), BF),
+            pltpu.VMEM((chunk, half), BF),
+            pltpu.VMEM((2, 4, chunk, half), BF),
+            pltpu.VMEM((chunk, hidden_units), BF),
+            pltpu.VMEM((4, chunk, half), BF),
+            pltpu.VMEM((4, chunk, half), BF),
+            pltpu.VMEM((4, chunk, half), BF),
+            pltpu.VMEM((chunk // 2, half), BF),
+            pltpu.VMEM((chunk // 2, half), BF),
+            pltpu.VMEM((chunk, half), BF),
+            pltpu.VMEM((chunk, half), BF),
+            pltpu.VMEM((chunk, half), F32),
+            pltpu.VMEM((chunk, half), BF),
+            pltpu.VMEM((tokens, half), F32),
+            pltpu.VMEM((tokens, half), F32),
+            dma((6,)), dma((3,)), dma((3,)), dma((n_ex,)), dma((n_ex,)), dma((2, 4)), dma((2, 4)),
+            dma((4,)), dma((4,)), dma((4, 4)), dma((4, 4)), dma((4,)), dma((4,)),
+            dma((4,)), dma((4,)), dma((2, 4)), dma((2, 4)), dma((n_ex,)), dma((n_ex,)),
+        ],
+        compiler_params=pltpu.CompilerParams(
+            collective_id=1, has_side_effects=True, vmem_limit_bytes=60 * 2**20
+        ),
+    )(
+        residual.reshape(tokens, width), normed.reshape(tokens, width), jnp.swapaxes(expert_ids, 1, 2), router.T,
+        w_in.reshape(width, hidden_units), w_out.reshape(hidden_units, width),
     )
-    returned = lax.all_to_all(
-        summed.reshape(expert_count, stack_size * capacity, width),
-        "expert",
-        split_axis=0,
-        concat_axis=0,
-        tiled=True,
-    )
-    gathered = jnp.dot(
-        dispatch, returned.reshape(columns, width), preferred_element_type=jnp.float32
-    )
-    return gathered.reshape(stack_size, row_count, top_count, width)
-
-
-def finish(residual, normed, chosen_ids, router, w_in, w_out):
-    expert_count = router.shape[1]
-    logits = jnp.einsum("srd,de->sre", normed, router, preferred_element_type=jnp.float32)
-    match_table = (
-        chosen_ids[:, :, :, None] == jnp.arange(expert_count, dtype=jnp.int32)[None, None, None, :]
-    )
-    chosen = jnp.sum(jnp.where(match_table, logits[:, :, None, :], 0.0), axis=3)
-    first_gate = jax.nn.sigmoid(chosen[:, :, 0] - chosen[:, :, 1])
-    gate_mix = jnp.stack([first_gate, 1.0 - first_gate], axis=2)
-    expert_out = experts_apply(normed, chosen_ids, w_in, w_out)
-    return (residual + jnp.sum(gate_mix[:, :, :, None] * expert_out, axis=2)).astype(jnp.bfloat16)
 
 
 def shards(
@@ -479,7 +746,7 @@
         hidden, q_self, k_new, v_new, q_cross, cache_keys, cache_values, cross_keys, cross_values,
         key_scale, value_scale, parents, norm_gain,
     )
-    return finish(residual, normed, expert_ids, router, w_in, w_out)
+    return experts(residual, normed, expert_ids, router, w_in, w_out)
 
 
 def solution(mesh):

time: 172 us -> 94.4 us (0.55)
  the two profiles are of different devices: /device:TPU:0 before, /device:TPU:1 now
where the time goes in v2:
time: 94.4 us; the launch traced here: 94.2 us
  Pallas kernels  92.6 us (98%)
  local copies, waits for them, and re-layouts  1.57 us (2%)
    pallas_call x1, Pallas kernels, experts(): pl.pallas_call(functools.partial(experts_kernel, n_dp, n_ex, cap), out_sh...  65.8 us
    pallas_call x1, Pallas kernels, attention(): pl.pallas_call(functools.partial(attention_kernel, n_dp, n_ex, rows, cach...  26.8 us

profile of v2, /device:TPU:1, one launch (start us, length us, event | category | flops | bytes accessed | tf_op | source)
XLA Modules:
  0.0 94.2 jit_solution(13933783345467484277)
XLA Ops:
  0.0 26.8 %shard_map.163 = (f32[2,16,2048]{2,1,0:T(8,128)}, bf16[2,16,2048]{2,1,0:T(8,128)(2,1)}) custom-call(bf16[2,16,2048]{2,1,0:T(8,128)(2,1)} %hidden_hbm.1, bf16[2,16,2048]{2,1,0:T(8,128)(2,1)} %q_self_hbm.1, bf16[2,16,2048]{2,1,0:T(8,128)(2,1)} %k_new_hbm.1, bf16[2,16,2048]{2,1,0:T(8,128)(2,1)} %v_new_hbm.1, bf16[2,16,2048]{2,1,0:T(8,128)(2,1)} %q_cross_hbm.1, ...), custom_call_target="tpu_custom_call" | custom-call | tf_op jit(solution)/shard_map/pallas_call | solution.py:365
  26.8 65.8 %shard_map.164 = bf16[2,16,2048]{2,1,0:T(8,128)(2,1)} custom-call(f32[32,2048]{1,0:T(8,128)} %bitcast.17, bf16[32,2048]{1,0:T(8,128)(2,1)} %bitcast.18, s32[2,2,16]{2,1,0:T(2,128)} %bitcast.21, bf16[16,2048]{1,0:T(8,128)(2,1)} %bitcast.19, bf16[2048,1024]{1,0:T(8,128)(2,1)} %bitcast.15, bf16[1024,2048]{1,0:T(8,128)(2,1)} %bitcast.16), custom_call_target="tpu_custom_call" | custom-call | tf_op jit(solution)/shard_map/pallas_call | solution.py:701
  92.6 1.6 %copy.19 = bf16[2,16,2048]{2,1,0:T(8,128)(2,1)} copy(bf16[2,16,2048]{2,1,0:T(8,128)(2,1)} %shard_map.164) | data formatting | bytes 262144

commit v3 on v2

--- a/solution.py
+++ b/solution.py
@@ -48,16 +48,17 @@
     return lax.dot_general(a, b, (((1,), (1,)), ((), ())), preferred_element_type=F32)
 
 
-def attention_kernel(
-    n_dp, n_ex, rows, cache, src, beams, chunks,
-    hidden_hbm, q_self_hbm, k_new_hbm, v_new_hbm, q_cross_hbm, parents_hbm, ks_hbm, vs_hbm, gain_hbm,
-    ck_hbm, cv_hbm, xk_hbm, xv_hbm,
-    residual_ref, normed_ref,
+def attention_part(n_dp, n_ex, rows, cache, src, beams, chunks, inputs, scratch, residual, normed, first_row, enter):
+    (
+        hidden_hbm, q_self_hbm, k_new_hbm, v_new_hbm, q_cross_hbm, parents_hbm, ks_hbm, vs_hbm, gain_hbm,
+        ck_hbm, cv_hbm, xk_hbm, xv_hbm,
+    ) = inputs
+    (
     hidden, q_self, k_new, v_new, q_cross, parents, key_scale, value_scale, gain,
     kbuf, vbuf, xkbuf, xvbuf, q_all, o_all, o_send, x_out, bias, bias_e, bias_x, scales,
     stat, par_own, par_in, q_d, q_e, in_c, in_d, in_e, o_d, o_e, back_c, back_d, back_e, stat_in, stat_in2,
-    load_sem, small_sem, send_sem, recv_sem,
-):
+    s_self, w_self, s_cross, w_cross, load_sem, small_sem, send_sem, recv_sem,
+    ) = scratch
     width = hidden.shape[2]
     heads = key_scale.shape[1]
     size = width // heads
@@ -69,10 +70,6 @@
     def at(offset):
         other = lax.rem(me + offset + n_dev, n_dev)
         return (other // n_ex, lax.rem(other, n_ex))
-
-    barrier = pltpu.get_barrier_semaphore()
-    for offset in (-1, -2, 1, 2):
-        pl.semaphore_signal(barrier, inc=1, device_id=at(offset), device_id_type=MESH)
 
     def load(k, c, source, buffer):
         part = width // chunks
@@ -90,10 +87,14 @@
     ]
     for copy in small:
         copy.start()
+    early = chunks // 2
+    for c in range(early):
+        load(2, c, xk_hbm, xkbuf).start()
+        load(3, c, xv_hbm, xvbuf).start()
     for c in range(chunks):
         load(0, c, ck_hbm, kbuf).start()
         load(1, c, cv_hbm, vbuf).start()
-    for c in range(chunks):
+    for c in range(early, chunks):
         load(2, c, xk_hbm, xkbuf).start()
         load(3, c, xv_hbm, xvbuf).start()
 
@@ -136,7 +137,7 @@
         remote(q_e, in_e, 3, -2),
         remote(q_self.at[1], in_c, 4, -1),
     ]
-    pl.semaphore_wait(barrier, 4)
+    enter()
     for copy in out_copies:
         copy.start()
 
@@ -155,10 +156,33 @@
     bias_x[...] = jnp.where(
         iota((2 * rows, n_cross), 1) // src == (iota((2 * rows, n_cross), 0) & (rows - 1)) // beams, 0.0, LOW
     )
+    def cross_chunk(c, carry):
+        load(2, c, xk_hbm, xkbuf).wait()
+        load(3, c, xv_hbm, xvbuf).wait()
+        lanes_x = iota((2 * rows, 128), 1)
+        heads_at = [pl.ds(pl.multiple_of((c * per_chunk + j) * size, size), size) for j in range(per_chunk)]
+        for j in range(per_chunk):
+            ks_h = jnp.sum(jnp.where(lanes_x == c * per_chunk + j, scales[0], 0.0), axis=1, keepdims=True)
+            q = jnp.concatenate([q_cross[0, :, heads_at[j]], q_cross[1, :, heads_at[j]]], axis=0)
+            s_cross[j] = tdot(q, xkbuf[c, :, j * size:(j + 1) * size]) * ks_h + bias_x[...]
+        totals = []
+        for j in range(per_chunk):
+            s = s_cross[j]
+            w = jnp.exp(s - jnp.max(s, axis=1, keepdims=True))
+            totals.append(jnp.sum(w, axis=1, keepdims=True))
+            w_cross[j] = w.astype(BF)
+        for j in range(per_chunk):
+            vs_h = jnp.sum(jnp.where(lanes_x == c * per_chunk + j, scales[1], 0.0), axis=1, keepdims=True)
+            o = bdot(w_cross[j], xvbuf[c, :, j * size:(j + 1) * size])
+            x_out[:, heads_at[j]] = o * (vs_h / totals[j])
+        return carry
+
+    small[6].wait()
+    lax.fori_loop(0, early, cross_chunk, 0)
     q_all[0:rows, :] = q_self[0]
     q_all[rows:2 * rows, :] = q_self[1]
 
-    for i in (2, 3, 6, 7, 8):
+    for i in (2, 3, 7, 8):
         small[i].wait()
     for copy in out_copies:
         copy.wait()
@@ -220,24 +244,31 @@
     def self_chunk(c, carry):
         load(0, c, ck_hbm, kbuf).wait()
         load(1, c, cv_hbm, vbuf).wait()
+        heads_at = [pl.ds(pl.multiple_of((c * per_chunk + j) * size, size), size) for j in range(per_chunk)]
+        extras = []
         for j in range(per_chunk):
-            h = c * per_chunk + j
-            at_h = pl.ds(pl.multiple_of(h * size, size), size)
-            q = q_all[:, at_h]
-            k_extra = jnp.concatenate([k_new[0, :, at_h], k_new[1, :, at_h]], axis=0)
-            v_extra = jnp.concatenate([v_new[0, :, at_h], v_new[1, :, at_h]], axis=0)
-            s = tdot(q, kbuf[c, :, j * size:(j + 1) * size]) * root + bias[...]
-            s_e = tdot(q, k_extra) * root + bias_e[...]
+            q = q_all[:, heads_at[j]]
+            k_extra = jnp.concatenate([k_new[0, :, heads_at[j]], k_new[1, :, heads_at[j]]], axis=0)
+            s_self[j] = tdot(q, kbuf[c, :, j * size:(j + 1) * size]) * root + bias[...]
+            extras.append(tdot(q, k_extra) * root + bias_e[...])
+        for j in range(per_chunk):
+            s, s_e = s_self[j], extras[j]
             top = jnp.maximum(
                 jnp.maximum(jnp.max(s, axis=1, keepdims=True), jnp.max(s_e, axis=1, keepdims=True)), FLOOR
             )
             w = jnp.exp(s - top)
             w_e = jnp.exp(s_e - top)
             total = jnp.sum(w, axis=1, keepdims=True) + jnp.sum(w_e, axis=1, keepdims=True)
-            o = bdot(w.astype(BF), vbuf[c, :, j * size:(j + 1) * size]) + bdot(w_e.astype(BF), v_extra)
-            o_all[:, at_h] = o
-            stat[0] = jnp.where(lanes == h, top, stat[0])
-            stat[1] = jnp.where(lanes == h, total, stat[1])
+            w_self[j] = w.astype(BF)
+            extras[j] = w_e.astype(BF)
+            here = lanes == c * per_chunk + j
+            stat[0] = jnp.where(here, top, stat[0])
+            stat[1] = jnp.where(here, total, stat[1])
+        for j in range(per_chunk):
+            v_extra = jnp.concatenate([v_new[0, :, heads_at[j]], v_new[1, :, heads_at[j]]], axis=0)
+            o_all[:, heads_at[j]] = bdot(w_self[j], vbuf[c, :, j * size:(j + 1) * size]) + bdot(
+                extras[j], v_extra
+            )
         return carry
 
     lax.fori_loop(0, chunks, self_chunk, 0)
@@ -263,25 +294,7 @@
     for copy in back_copies:
         copy.start()
 
-    def cross_chunk(c, carry):
-        load(2, c, xk_hbm, xkbuf).wait()
-        load(3, c, xv_hbm, xvbuf).wait()
-        for j in range(per_chunk):
-            h = c * per_chunk + j
-            at_h = pl.ds(pl.multiple_of(h * size, size), size)
-            lanes_x = iota((2 * rows, 128), 1)
-            ks_h = jnp.sum(jnp.where(lanes_x == h, scales[0], 0.0), axis=1, keepdims=True)
-            vs_h = jnp.sum(jnp.where(lanes_x == h, scales[1], 0.0), axis=1, keepdims=True)
-            q = jnp.concatenate([q_cross[0, :, at_h], q_cross[1, :, at_h]], axis=0)
-            s = tdot(q, xkbuf[c, :, j * size:(j + 1) * size]) * ks_h + bias_x[...]
-            top = jnp.max(s, axis=1, keepdims=True)
-            w = jnp.exp(s - top)
-            total = jnp.sum(w, axis=1, keepdims=True)
-            o = bdot(w.astype(BF), xvbuf[c, :, j * size:(j + 1) * size])
-            x_out[:, at_h] = o * (vs_h / total)
-        return carry
-
-    lax.fori_loop(0, chunks, cross_chunk, 0)
+    lax.fori_loop(early, chunks, cross_chunk, 0)
 
     for copy in back_copies:
         copy.wait()
@@ -338,94 +351,27 @@
                     + back_c[:, at_h].astype(F32) * w1[1][:, h:h + 1]
                     + o_far1[k][:, inner] * w1[2][:, h:h + 1]
                 )
-            residual_ref[t, :, at_h] = (
+            residual[t * rows:(t + 1) * rows, at_h] = (
                 hidden[t, :, at_h].astype(F32) + mixed + x_out[t * rows:(t + 1) * rows, at_h]
             )
-    for t in range(2):
-        value = residual_ref[t]
-        average = jnp.mean(value, axis=1, keepdims=True)
-        centered = value - average
-        variance = jnp.mean(centered * centered, axis=1, keepdims=True)
-        normed_ref[t] = (centered * lax.rsqrt(variance + epsilon) * gain[...]).astype(BF)
-
-
-def attention(hidden, q_self, k_new, v_new, q_cross, cache_keys, cache_values, cross_keys, cross_values,
-              key_scale, value_scale, parents, norm_gain):
-    steps, rows, width = hidden.shape
-    heads = key_scale.shape[1]
-    cache = cache_keys.shape[1]
-    sentences, src = cross_keys.shape[:2]
-    chunks = 4
-    n_dp, n_ex = lax.axis_size("dp"), lax.axis_size("expert")
-    part = width // chunks
-    n_self, n_cross, slots = rows * cache, sentences * src, 4 * rows
-    vmem = pl.BlockSpec(memory_space=pltpu.VMEM)
-    hbm = pl.BlockSpec(memory_space=pl.ANY)
-    quarter = width // 4
-    return pl.pallas_call(
-        functools.partial(attention_kernel, n_dp, n_ex, rows, cache, src, rows // sentences, chunks),
-        out_shape=(
-            jax.ShapeDtypeStruct((steps, rows, width), F32),
-            jax.ShapeDtypeStruct((steps, rows, width), BF),
-        ),
-        in_specs=[hbm] * 13,
-        out_specs=(vmem, vmem),
-        scratch_shapes=[pltpu.VMEM((steps, rows, width), BF)] * 5 + [
-            pltpu.VMEM((steps, rows), jnp.int32),
-            pltpu.VMEM((sentences, heads), F32),
-            pltpu.VMEM((sentences, heads), F32),
-            pltpu.VMEM((1, width), F32),
-            pltpu.VMEM((chunks, n_self, part), BF),
-            pltpu.VMEM((chunks, n_self, part), BF),
-            pltpu.VMEM((chunks, n_cross, part), BF),
-            pltpu.VMEM((chunks, n_cross, part), BF),
-            pltpu.VMEM((slots, width), BF),
-            pltpu.VMEM((slots, width), F32),
-            pltpu.VMEM((2 * rows, width), BF),
-            pltpu.VMEM((2 * rows, width), F32),
-            pltpu.VMEM((slots, n_self), F32),
-            pltpu.VMEM((slots, 2 * rows), F32),
-            pltpu.VMEM((2 * rows, n_cross), F32),
-            pltpu.VMEM((2, 2 * rows, 128), F32),
-            pltpu.VMEM((2, slots, 128), F32),
-            pltpu.VMEM((8, 128), jnp.int32),
-            pltpu.VMEM((2, 8, 128), jnp.int32),
-            pltpu.VMEM((16, quarter), BF),
-            pltpu.VMEM((16, quarter), BF),
-            pltpu.VMEM((rows, width), BF),
-            pltpu.VMEM((16, quarter), BF),
-            pltpu.VMEM((16, quarter), BF),
-            pltpu.VMEM((16, quarter), BF),
-            pltpu.VMEM((16, quarter), BF),
-            pltpu.VMEM((rows, width), BF),
-            pltpu.VMEM((16, quarter), BF),
-            pltpu.VMEM((16, quarter), BF),
-            pltpu.VMEM((2, rows + 8, 128), F32),
-            pltpu.VMEM((2, 8, 128), F32),
-            pltpu.SemaphoreType.DMA((4, chunks)),
-            pltpu.SemaphoreType.DMA((9,)),
-            pltpu.SemaphoreType.DMA((10,)),
-            pltpu.SemaphoreType.DMA((10,)),
-        ],
-        compiler_params=pltpu.CompilerParams(
-            collective_id=0, has_side_effects=True, vmem_limit_bytes=60 * 2**20
-        ),
-    )(
-        hidden, q_self, k_new, v_new, q_cross, parents, key_scale, value_scale, norm_gain.reshape(1, width),
-        cache_keys.reshape(n_self, width), cache_values.reshape(n_self, width),
-        cross_keys.reshape(n_cross, width), cross_values.reshape(n_cross, width),
-    )
-
-
-def experts_kernel(
+    value = residual[...]
+    average = jnp.mean(value, axis=1, keepdims=True)
+    centered = value - average
+    variance = jnp.mean(centered * centered, axis=1, keepdims=True)
+    normed[first_row, :] = (centered * lax.rsqrt(variance + epsilon) * gain[...]).astype(BF)
+
+
+def layer_kernel(
     n_dp, n_ex, cap,
-    residual_hbm, normed_hbm, ids_hbm, router_hbm, w_in_hbm, w_out_hbm,
-    out_ref,
+    inputs, attention_args, scratch, out_ref,
+):
+    ids_hbm, router_hbm, w_in_hbm, w_out_hbm = inputs
+    (
     residual, normed, ids, ids_all, router, w_in, w_out, outgoing, xbuf, units, p_mine, p_send, p_back,
     rs_a, rs_b, fin_a, fin_b, home, returned, y_send, y_back,
     load_sem, pair_s, pair_r, a2a_s, a2a_r, near_s, near_r, fwd_s, fwd_r, sib_s, sib_r, part_s, part_r,
     rs_s, rs_r, fin_s, fin_r, ret_s, ret_r,
-):
+    ) = scratch
     steps, rows = ids.shape[0], ids.shape[2]
     tokens = steps * rows
     width = residual.shape[1]
@@ -450,22 +396,31 @@
         return (dp, lax.rem(me - o + n_ex, n_ex))
 
     barrier = pltpu.get_barrier_semaphore()
-    others = [sibling, up_y, down_y] + [peer(o) for o in range(1, n_ex)]
+    position = dp * n_ex + me
+
+    def along(offset):
+        other = lax.rem(position + offset + n_dp * n_ex, n_dp * n_ex)
+        return (other // n_ex, lax.rem(other, n_ex))
+
+    others = [sibling, up_y, down_y] + [peer(o) for o in range(1, n_ex)] + [along(o) for o in (-1, -2, 1, 2)]
     for other in others:
         pl.semaphore_signal(barrier, inc=1, device_id=other, device_id_type=MESH)
 
     mine = pl.ds(pl.multiple_of(core * tokens, tokens), tokens)
     theirs = pl.ds(pl.multiple_of((1 - core) * tokens, tokens), tokens)
     loads = [
-        pltpu.make_async_copy(normed_hbm, normed.at[mine], load_sem.at[0]),
-        pltpu.make_async_copy(ids_hbm, ids, load_sem.at[1]),
-        pltpu.make_async_copy(router_hbm, router, load_sem.at[2]),
-        pltpu.make_async_copy(w_in_hbm, w_in, load_sem.at[3]),
-        pltpu.make_async_copy(w_out_hbm, w_out, load_sem.at[4]),
-        pltpu.make_async_copy(residual_hbm, residual, load_sem.at[5]),
+        pltpu.make_async_copy(ids_hbm, ids, load_sem.at[0]),
+        pltpu.make_async_copy(router_hbm, router, load_sem.at[1]),
+        pltpu.make_async_copy(w_in_hbm, w_in, load_sem.at[2]),
+        pltpu.make_async_copy(w_out_hbm, w_out, load_sem.at[3]),
     ]
-    for copy in loads:
-        copy.start()
+
+    def enter():
+        for copy in loads:
+            copy.start()
+        pl.semaphore_wait(barrier, len(others))
+
+    attention_part(n_dp, n_ex, *attention_args, residual, normed, mine, enter)
 
     started = []
 
@@ -479,11 +434,9 @@
         return copy
 
     loads[0].wait()
-    loads[1].wait()
     for t in range(steps):
         named = [as_column(ids[t, k:k + 1, :].astype(F32), rows).astype(jnp.int32) for k in range(2)]
         ids_all[core, t * rows:(t + 1) * rows, :] = jnp.where(iota((rows, 128), 1) == 0, named[0], named[1])
-    pl.semaphore_wait(barrier, len(others))
     pair = [
         send(normed.at[mine], normed.at[mine], pair_s.at[0], pair_r.at[0], sibling),
         send(ids_all.at[core], ids_all.at[core], pair_s.at[1], pair_r.at[1], sibling),
@@ -527,7 +480,7 @@
         )
     xbuf[core, 0, block(0), :] = outgoing[block(0), :]
 
-    loads[2].wait()
+    loads[1].wait()
     logits = tdot(normed[...], router[...])
     lane_e = iota((tokens, n_ex), 1)
     gates = []
@@ -590,8 +543,8 @@
         near[1, g] = send(xbuf.at[core, 0, piece(g)], xbuf.at[core, 1, piece(g)], near_s.at[0, g], near_r.at[0, g], up_y)
         near[2, g] = send(xbuf.at[core, 0, piece(g)], xbuf.at[core, 2, piece(g)], near_s.at[1, g], near_r.at[1, g], down_y)
         sib[0, g] = to_sibling(0, g)
+    loads[2].wait()
     loads[3].wait()
-    loads[4].wait()
     for g in range(4):
         sib[0, g].wait_recv()
     parts = [compute(0)]
@@ -673,7 +626,6 @@
     y_send[...] = jnp.where(is_first, ys[1], ys[0])
     swap = send(y_send, y_back, pair_s.at[2], pair_r.at[2], sibling)
     own_y = jnp.where(is_first, ys[0], ys[1])
-    loads[5].wait()
     residual[:, at_half] = residual[:, at_half] + own_y
     swap.wait_recv()
     at_other = pl.ds(pl.multiple_of((1 - core) * half, half), half)
@@ -686,24 +638,65 @@
             copy.wait_send()
 
 
-def experts(residual, normed, expert_ids, router, w_in, w_out):
-    steps, rows, width = residual.shape
+def layer(hidden, q_self, k_new, v_new, q_cross, cache_keys, cache_values, cross_keys, cross_values,
+          key_scale, value_scale, parents, expert_ids, norm_gain, router, w_in, w_out):
+    steps, rows, width = hidden.shape
+    heads = key_scale.shape[1]
+    cache = cache_keys.shape[1]
+    sentences, src = cross_keys.shape[:2]
+    chunks = 4
     n_dp, n_ex = lax.axis_size("dp"), lax.axis_size("expert")
+    part = width // chunks
+    n_self, n_cross, slots = rows * cache, sentences * src, 4 * rows
+    quarter = width // 4
     tokens = steps * rows
     hidden_units = w_in.shape[2]
     half = width // 2
     cap = 4 * rows // n_ex
-    slots = 2 * steps * cap
-    chunk = n_ex * slots
-    vmem = pl.BlockSpec(memory_space=pltpu.VMEM)
-    hbm = pl.BlockSpec(memory_space=pl.ANY)
+    chunk_slots = n_ex * 2 * steps * cap
     dma = pltpu.SemaphoreType.DMA
-    return pl.pallas_call(
-        functools.partial(experts_kernel, n_dp, n_ex, cap),
-        out_shape=jax.ShapeDtypeStruct((steps, rows, width), BF),
-        in_specs=[hbm] * 6,
-        out_specs=vmem,
-        scratch_shapes=[
+    attention_scratch = [pltpu.VMEM((steps, rows, width), BF)] * 5 + [
+            pltpu.VMEM((steps, rows), jnp.int32),
+            pltpu.VMEM((sentences, heads), F32),
+            pltpu.VMEM((sentences, heads), F32),
+            pltpu.VMEM((1, width), F32),
+            pltpu.VMEM((chunks, n_self, part), BF),
+            pltpu.VMEM((chunks, n_self, part), BF),
+            pltpu.VMEM((chunks, n_cross, part), BF),
+            pltpu.VMEM((chunks, n_cross, part), BF),
+            pltpu.VMEM((slots, width), BF),
+            pltpu.VMEM((slots, width), F32),
+            pltpu.VMEM((2 * rows, width), BF),
+            pltpu.VMEM((2 * rows, width), F32),
+            pltpu.VMEM((slots, n_self), F32),
+            pltpu.VMEM((slots, 2 * rows), F32),
+            pltpu.VMEM((2 * rows, n_cross), F32),
+            pltpu.VMEM((2, 2 * rows, 128), F32),
+            pltpu.VMEM((2, slots, 128), F32),
+            pltpu.VMEM((8, 128), jnp.int32),
+            pltpu.VMEM((2, 8, 128), jnp.int32),
+            pltpu.VMEM((16, quarter), BF),
+            pltpu.VMEM((16, quarter), BF),
+            pltpu.VMEM((rows, width), BF),
+            pltpu.VMEM((16, quarter), BF),
+            pltpu.VMEM((16, quarter), BF),
+            pltpu.VMEM((16, quarter), BF),
+            pltpu.VMEM((16, quarter), BF),
+            pltpu.VMEM((rows, width), BF),
+            pltpu.VMEM((16, quarter), BF),
+            pltpu.VMEM((16, quarter), BF),
+            pltpu.VMEM((2, rows + 8, 128), F32),
+            pltpu.VMEM((2, 8, 128), F32),
+            pltpu.VMEM((heads // chunks, slots, n_self), F32),
+            pltpu.VMEM((heads // chunks, slots, n_self), BF),
+            pltpu.VMEM((heads // chunks, 2 * rows, n_cross), F32),
+            pltpu.VMEM((heads // chunks, 2 * rows, n_cross), BF),
+            pltpu.SemaphoreType.DMA((4, chunks)),
+            pltpu.SemaphoreType.DMA((9,)),
+            pltpu.SemaphoreType.DMA((10,)),
+            pltpu.SemaphoreType.DMA((10,)),
+        ]
+    expert_scratch = [
             pltpu.VMEM((tokens, width), F32),
             pltpu.VMEM((2 * tokens, width), BF),
             pltpu.VMEM((steps, 2, rows), jnp.int32),
@@ -711,42 +704,46 @@
             pltpu.VMEM((n_ex, width), BF),
             pltpu.VMEM((width, hidden_units), BF),
             pltpu.VMEM((hidden_units, width), BF),
-            pltpu.VMEM((chunk, half), BF),
-            pltpu.VMEM((2, 4, chunk, half), BF),
-            pltpu.VMEM((chunk, hidden_units), BF),
-            pltpu.VMEM((4, chunk, half), BF),
-            pltpu.VMEM((4, chunk, half), BF),
-            pltpu.VMEM((4, chunk, half), BF),
-            pltpu.VMEM((chunk // 2, half), BF),
-            pltpu.VMEM((chunk // 2, half), BF),
-            pltpu.VMEM((chunk, half), BF),
-            pltpu.VMEM((chunk, half), BF),
-            pltpu.VMEM((chunk, half), F32),
-            pltpu.VMEM((chunk, half), BF),
+            pltpu.VMEM((chunk_slots, half), BF),
+            pltpu.VMEM((2, 4, chunk_slots, half), BF),
+            pltpu.VMEM((chunk_slots, hidden_units), BF),
+            pltpu.VMEM((4, chunk_slots, half), BF),
+            pltpu.VMEM((4, chunk_slots, half), BF),
+            pltpu.VMEM((4, chunk_slots, half), BF),
+            pltpu.VMEM((chunk_slots // 2, half), BF),
+            pltpu.VMEM((chunk_slots // 2, half), BF),
+            pltpu.VMEM((chunk_slots, half), BF),
+            pltpu.VMEM((chunk_slots, half), BF),
+            pltpu.VMEM((chunk_slots, half), F32),
+            pltpu.VMEM((chunk_slots, half), BF),
             pltpu.VMEM((tokens, half), F32),
             pltpu.VMEM((tokens, half), F32),
-            dma((6,)), dma((3,)), dma((3,)), dma((n_ex,)), dma((n_ex,)), dma((2, 4)), dma((2, 4)),
+            dma((4,)), dma((3,)), dma((3,)), dma((n_ex,)), dma((n_ex,)), dma((2, 4)), dma((2, 4)),
             dma((4,)), dma((4,)), dma((4, 4)), dma((4, 4)), dma((4,)), dma((4,)),
             dma((4,)), dma((4,)), dma((2, 4)), dma((2, 4)), dma((n_ex,)), dma((n_ex,)),
-        ],
+        ]
+    def kernel(*refs):
+        layer_kernel(
+            n_dp, n_ex, cap, refs[13:17],
+            (rows, cache, src, rows // sentences, chunks, refs[0:13], refs[18]), refs[19], refs[17],
+        )
+
+    return pl.pallas_call(
+        kernel,
+        out_shape=jax.ShapeDtypeStruct((steps, rows, width), BF),
+        in_specs=[pl.BlockSpec(memory_space=pl.ANY)] * 17,
+        out_specs=pl.BlockSpec(memory_space=pltpu.VMEM),
+        scratch_shapes=(tuple(attention_scratch), tuple(expert_scratch)),
         compiler_params=pltpu.CompilerParams(
-            collective_id=1, has_side_effects=True, vmem_limit_bytes=60 * 2**20
+            collective_id=0, has_side_effects=True, vmem_limit_bytes=60 * 2**20
         ),
     )(
-        residual.reshape(tokens, width), normed.reshape(tokens, width), jnp.swapaxes(expert_ids, 1, 2), router.T,
+        hidden, q_self, k_new, v_new, q_cross, parents, key_scale, value_scale, norm_gain.reshape(1, width),
+        cache_keys.reshape(n_self, width), cache_values.reshape(n_self, width),
+        cross_keys.reshape(n_cross, width), cross_values.reshape(n_cross, width),
+        jnp.swapaxes(expert_ids, 1, 2), router.T,
         w_in.reshape(width, hidden_units), w_out.reshape(hidden_units, width),
     )
-
-
-def shards(
-    hidden, q_self, k_new, v_new, q_cross, cache_keys, cache_values, cross_keys, cross_values,
-    key_scale, value_scale, parents, expert_ids, norm_gain, router, w_in, w_out,
-):
-    residual, normed = attention(
-        hidden, q_self, k_new, v_new, q_cross, cache_keys, cache_values, cross_keys, cross_values,
-        key_scale, value_scale, parents, norm_gain,
-    )
-    return experts(residual, normed, expert_ids, router, w_in, w_out)
 
 
 def solution(mesh):
@@ -770,4 +767,4 @@
         P("expert", "dp", None),
     )
     out_specs = P(None, ("dp", "expert"), None)
-    return jax.shard_map(shards, mesh=mesh, in_specs=in_specs, out_specs=out_specs, check_vma=False)
+    return jax.shard_map(layer, mesh=mesh, in_specs=in_specs, out_specs=out_specs, check_vma=False)

time: 94.4 us -> 87.9 us (0.931)
  Pallas kernels: 92.6 us -> 86.3 us
    pallas_call x2 -> x1, Pallas kernels: 92.6 us -> 86.3 us  [layer(): pl.pallas_call(kernel, out_shape=jax.ShapeDtypeStruct((steps, rows, width...]
where the time goes in v3:
time: 87.9 us; the launch traced here: 87.8 us
  Pallas kernels  86.3 us (98%)
  local copies, waits for them, and re-layouts  1.57 us (2%)
    pallas_call x1, Pallas kernels, layer(): pl.pallas_call(kernel, out_shape=jax.ShapeDtypeStruct((steps, rows, width...  86.3 us

profile of v3, /device:TPU:1, one launch (start us, length us, event | category | flops | bytes accessed | tf_op | source)
XLA Modules:
  0.0 87.8 jit_solution(3353732801791105552)
XLA Ops:
  0.0 86.3 %shard_map.163 = bf16[2,16,2048]{2,1,0:T(8,128)(2,1)} custom-call(bf16[2,16,2048]{2,1,0:T(8,128)(2,1)} %refs_0_.1, bf16[2,16,2048]{2,1,0:T(8,128)(2,1)} %refs_1_.1, bf16[2,16,2048]{2,1,0:T(8,128)(2,1)} %refs_2_.1, bf16[2,16,2048]{2,1,0:T(8,128)(2,1)} %refs_3_.1, bf16[2,16,2048]{2,1,0:T(8,128)(2,1)} %refs_4_.1, s32[2,16]{1,0:T(2,128)} %refs_5_.1, ...), custom_call_target="tpu_custom_call" | custom-call | tf_op jit(solution)/shard_map/pallas_call | solution.py:731
  86.3 1.6 %copy.19 = bf16[2,16,2048]{2,1,0:T(8,128)(2,1)} copy(bf16[2,16,2048]{2,1,0:T(8,128)(2,1)} %shard_map.163) | data formatting | bytes 262144

commit v4 on v3

--- a/solution.py
+++ b/solution.py
@@ -367,10 +367,11 @@
 ):
     ids_hbm, router_hbm, w_in_hbm, w_out_hbm = inputs
     (
-    residual, normed, ids, ids_all, router, w_in, w_out, outgoing, xbuf, units, p_mine, p_send, p_back,
-    rs_a, rs_b, fin_a, fin_b, home, returned, y_send, y_back,
-    load_sem, pair_s, pair_r, a2a_s, a2a_r, near_s, near_r, fwd_s, fwd_r, sib_s, sib_r, part_s, part_r,
-    rs_s, rs_r, fin_s, fin_r, ret_s, ret_r,
+        residual, normed, ids, info, info_far, router, w_in, w_out, normed_far, outgoing, outgoing_far,
+        xbuf, units, p_mine, p_send, p_back, fin_a, fin_b, home, returned, returned_far,
+        far_out, far_in, y_send, y_back,
+        load_sem, pair_s, pair_r, far_s, far_r, a2a_s, a2a_r, far_a2a_s, far_a2a_r, near_s, near_r, sib_s, sib_r,
+        part_s, part_r, fin_s, fin_r, ret_s, ret_r, far_ret_s, far_ret_r,
     ) = scratch
     steps, rows = ids.shape[0], ids.shape[2]
     tokens = steps * rows
@@ -388,6 +389,8 @@
     sibling = (dp + 1 - 2 * core, me)
     up_y = (lax.rem(place + 1, n_y) * 2 + core, me)
     down_y = (lax.rem(place + n_y - 1, n_y) * 2 + core, me)
+    far_place = lax.rem(place + 2, n_y) * 2
+    far_same = (far_place + core, me)
 
     def peer(o):
         return (dp, lax.rem(me + o, n_ex))
@@ -402,12 +405,15 @@
         other = lax.rem(position + offset + n_dp * n_ex, n_dp * n_ex)
         return (other // n_ex, lax.rem(other, n_ex))
 
-    others = [sibling, up_y, down_y] + [peer(o) for o in range(1, n_ex)] + [along(o) for o in (-1, -2, 1, 2)]
+    others = (
+        [sibling, up_y, down_y, (far_place, me), (far_place + 1, me)]
+        + [peer(o) for o in range(1, n_ex)]
+        + [along(o) for o in (-1, -2, 1, 2)]
+    )
     for other in others:
         pl.semaphore_signal(barrier, inc=1, device_id=other, device_id_type=MESH)
 
     mine = pl.ds(pl.multiple_of(core * tokens, tokens), tokens)
-    theirs = pl.ds(pl.multiple_of((1 - core) * tokens, tokens), tokens)
     loads = [
         pltpu.make_async_copy(ids_hbm, ids, load_sem.at[0]),
         pltpu.make_async_copy(router_hbm, router, load_sem.at[1]),
@@ -433,70 +439,100 @@
         started.append(copy)
         return copy
 
+    pair = [send(normed.at[mine], normed.at[mine], pair_s.at[0], pair_r.at[0], sibling)]
+    far = [
+        send(
+            normed.at[mine, pl.ds(c * half, half)], normed_far.at[mine], far_s.at[c], far_r.at[core], (far_place + c, me)
+        )
+        for c in range(2)
+    ]
+
     loads[0].wait()
-    for t in range(steps):
-        named = [as_column(ids[t, k:k + 1, :].astype(F32), rows).astype(jnp.int32) for k in range(2)]
-        ids_all[core, t * rows:(t + 1) * rows, :] = jnp.where(iota((rows, 128), 1) == 0, named[0], named[1])
-    pair = [
-        send(normed.at[mine], normed.at[mine], pair_s.at[0], pair_r.at[0], sibling),
-        send(ids_all.at[core], ids_all.at[core], pair_s.at[1], pair_r.at[1], sibling),
-    ]
-    for copy in pair:
-        copy.wait_recv()
-
-    lane_x = iota((tokens, 128), 1)
+    loads[1].wait()
+    logits = tdot(normed[mine, :], router[...])
+    lane_e = iota((tokens, n_ex), 1).astype(F32)
+    lane_i = iota((tokens, 128), 1)
+    named = [
+        jnp.concatenate([as_column(ids[t, k:k + 1, :].astype(F32), rows) for t in range(steps)], axis=0)
+        for k in range(2)
+    ]
+    picked = [jnp.sum(jnp.where(lane_e == n, logits, 0.0), axis=1, keepdims=True) for n in named]
+    first_gate = 1.0 / (1.0 + jnp.exp(picked[1] - picked[0]))
+    info[core] = jnp.where(lane_i == 0, named[0], jnp.where(lane_i == 1, named[1], first_gate))
+    pair.append(send(info.at[core], info.at[core], pair_s.at[1], pair_r.at[1], sibling))
+    for c in range(2):
+        far.append(send(info.at[core], info_far.at[core], far_s.at[2 + c], far_r.at[2 + core], (far_place + c, me)))
+
+    lane_x = iota((tokens, 128), 1).astype(F32)
     lower = (iota((tokens, tokens), 1) < iota((tokens, tokens), 0)) & (
         iota((tokens, tokens), 0) // rows == iota((tokens, tokens), 1) // rows
     )
     lower = jnp.where(lower, 1.0, 0.0).astype(BF)
-    step_of = (iota((tokens, 1), 0) // rows)
-    hots = []
-    for c in range(2):
-        named = [ids_all[c, :, k:k + 1] for k in range(2)]
-        one_hot = [lane_x == n for n in named]
-        count = jnp.where(one_hot[0] | one_hot[1], 1.0, 0.0).astype(BF)
-        before = bdot(lower, count)
-        pair_hot = []
-        for k in range(2):
-            spot = jnp.sum(jnp.where(one_hot[k], before, 0.0), axis=1, keepdims=True).astype(jnp.int32)
-            distance = named[k] - me
-            distance = jnp.where(distance < 0, distance + n_ex, distance)
-            column = distance * slots + (c * steps * cap + spot) + step_of * cap
-            pair_hot.append(iota((tokens, chunk), 1) == column)
-        hots.append(pair_hot)
-    dispatch = jnp.concatenate([jnp.where(h[0] | h[1], 1.0, 0.0).astype(BF) for h in hots], axis=0)
-    at_half = pl.ds(pl.multiple_of(core * half, half), half)
-    outgoing[...] = lax.dot_general(
-        dispatch, normed[:, at_half], (((0,), (0,)), ((), ())), preferred_element_type=F32
-    ).astype(BF)
+    step_of = (iota((tokens, 1), 0) // rows).astype(F32)
+    lane_c = iota((tokens, chunk), 1).astype(F32)
+    my_expert = me.astype(F32)
+
+    def routes(table):
+        hot_rows, gate_rows = [], []
+        for c in range(2):
+            named = [table[c, :, k:k + 1] for k in range(2)]
+            gate = table[c, :, 2:3]
+            one_hot = [lane_x == n for n in named]
+            before = bdot(lower, jnp.where(one_hot[0] | one_hot[1], 1.0, 0.0).astype(BF))
+            hots = []
+            for k in range(2):
+                spot = jnp.sum(jnp.where(one_hot[k], before, 0.0), axis=1, keepdims=True)
+                distance = named[k] - my_expert
+                distance = jnp.where(distance < 0.0, distance + n_ex, distance)
+                column = distance * slots + spot + step_of * cap + c * steps * cap
+                hots.append(lane_c == column)
+            hot_rows.append(jnp.where(hots[0] | hots[1], 1.0, 0.0).astype(BF))
+            gate_rows.append(jnp.where(hots[0], gate, 0.0) + jnp.where(hots[1], 1.0 - gate, 0.0))
+        gates = jnp.concatenate(gate_rows, axis=0)
+        high = gates.astype(BF)
+        return jnp.concatenate(hot_rows, axis=0), (high, (gates - high.astype(F32)).astype(BF))
+
+    def spread(hot, value):
+        return lax.dot_general(hot, value, (((0,), (0,)), ((), ())), preferred_element_type=F32).astype(BF)
 
     def block(o):
         return pl.ds(o * slots, slots)
 
-    arrivals = [None]
-    for o in range(1, n_ex):
-        arrivals.append(
-            send(outgoing.at[block(o)], xbuf.at[core, 0, block(o)], a2a_s.at[o], a2a_r.at[o], peer(o))
-        )
-    xbuf[core, 0, block(0), :] = outgoing[block(0), :]
-
-    loads[1].wait()
-    logits = tdot(normed[...], router[...])
-    lane_e = iota((tokens, n_ex), 1)
-    gates = []
-    for c in range(2):
-        part = logits[c * tokens:(c + 1) * tokens]
-        picked = [
-            jnp.sum(jnp.where(lane_e == ids_all[c, :, k:k + 1], part, 0.0), axis=1, keepdims=True)
-            for k in range(2)
-        ]
-        first = 1.0 / (1.0 + jnp.exp(picked[1] - picked[0]))
-        gates.append(
-            jnp.where(hots[c][0], first, 0.0) + jnp.where(hots[c][1], 1.0 - first, 0.0)
-        )
-
     def piece(g):
         return pl.ds(g * group, group)
+
+    at_half = pl.ds(pl.multiple_of(core * half, half), half)
+    for copy in pair:
+        copy.wait_recv()
+    dispatch, mix = routes(info)
+    outgoing[...] = spread(dispatch, normed[:, at_half])
+    arrivals = [None] + [
+        send(outgoing.at[block(o)], xbuf.at[core, 0, block(o)], a2a_s.at[o], a2a_r.at[o], peer(o))
+        for o in range(1, n_ex)
+    ]
+    xbuf[core, 0, block(0), :] = outgoing[block(0), :]
+    recv_far = [
+        pltpu.make_async_remote_copy(
+            src_ref=normed.at[mine, pl.ds(0, half)], dst_ref=normed_far.at[pl.ds(c * tokens, tokens)],
+            send_sem=far_s.at[c], recv_sem=far_r.at[c], device_id=far_same, device_id_type=MESH,
+        )
+        for c in range(2)
+    ] + [
+        pltpu.make_async_remote_copy(
+            src_ref=info.at[core], dst_ref=info_far.at[c],
+            send_sem=far_s.at[2 + c], recv_sem=far_r.at[2 + c], device_id=far_same, device_id_type=MESH,
+        )
+        for c in range(2)
+    ]
+    for copy in recv_far:
+        copy.wait_recv()
+    dispatch_far, mix_far = routes(info_far)
+    outgoing_far[...] = spread(dispatch_far, normed_far[...])
+    far_arrivals = [None] + [
+        send(outgoing_far.at[block(o)], xbuf.at[core, 3, block(o)], far_a2a_s.at[o], far_a2a_r.at[o], peer(o))
+        for o in range(1, n_ex)
+    ]
+    xbuf[core, 3, block(0), :] = outgoing_far[block(0), :]
 
     per_group = n_ex // 4
 
@@ -505,22 +541,26 @@
             xbuf.at[core, k, piece(g)], xbuf.at[core, k, piece(g)], sib_s.at[k, g], sib_r.at[k, g], sibling
         )
 
+    def from_near(k, g):
+        return 1 + g // 2, 2 * (k - 1) + g % 2
+
     tile = min(256, half, hidden_units)
 
-    def compute(k):
+    def first_product(k, slot):
         def first(j, carry):
             cols = pl.ds(pl.multiple_of(j * tile, tile), tile)
             a = bdot(xbuf[0, k], w_in[0:half, cols]) + bdot(xbuf[1, k], w_in[half:width, cols])
-            units[:, cols] = jnp.maximum(a, 0.0).astype(BF)
+            units[slot, :, cols] = jnp.maximum(a, 0.0).astype(BF)
             return carry
 
         lax.fori_loop(0, hidden_units // tile, first, 0)
 
+    def second_product(k, slot):
         def second(base, target):
             def step(j, carry):
                 cols = pl.ds(pl.multiple_of(base + j * tile, tile), tile)
                 target[k, :, pl.ds(pl.multiple_of(j * tile, tile), tile)] = bdot(
-                    units[...], w_out[:, cols]
+                    units[slot], w_out[:, cols]
                 ).astype(BF)
                 return carry
 
@@ -531,110 +571,118 @@
         second(core * half, p_mine)
         return copy
 
-    def reduce_part(k, g):
-        return p_mine[k, piece(g), :].astype(F32) + p_back[k, piece(g), :].astype(F32)
-
-    sib = {}
-    near = {}
+    def reduce_part(k):
+        return p_mine[k].astype(F32) + p_back[k].astype(F32)
+
+    sib, near, final = {}, {}, {}
     for g in range(4):
         for o in range(g * per_group, (g + 1) * per_group):
             if o:
                 arrivals[o].wait_recv()
-        near[1, g] = send(xbuf.at[core, 0, piece(g)], xbuf.at[core, 1, piece(g)], near_s.at[0, g], near_r.at[0, g], up_y)
-        near[2, g] = send(xbuf.at[core, 0, piece(g)], xbuf.at[core, 2, piece(g)], near_s.at[1, g], near_r.at[1, g], down_y)
+        for k in (1, 2):
+            to_chunk, spot = from_near(k, g)
+            near[k, g] = send(
+                xbuf.at[core, 0, piece(g)], xbuf.at[core, to_chunk, piece(spot)],
+                near_s.at[k - 1, g], near_r.at[k - 1, g], up_y if k == 1 else down_y,
+            )
         sib[0, g] = to_sibling(0, g)
     loads[2].wait()
     loads[3].wait()
     for g in range(4):
         sib[0, g].wait_recv()
-    parts = [compute(0)]
-    far = []
+    first_product(0, 0)
+    parts = {0: second_product(0, 0)}
+
+    def near_arrived(h):
+        for g in (2 * h, 2 * h + 1):
+            for k in (1, 2):
+                near[k, g].wait_recv()
+                to_chunk, spot = from_near(k, g)
+                sib[to_chunk, spot] = to_sibling(to_chunk, spot)
+
+    def finish_near(h):
+        parts[1 + h].wait()
+        p_send[1 + h] = reduce_part(1 + h).astype(BF)
+        for g in (2 * h, 2 * h + 1):
+            for k in (1, 2):
+                from_chunk, spot = from_near(k, g)
+                final[k, g] = send(
+                    p_send.at[from_chunk, piece(spot)], (fin_b if k == 1 else fin_a).at[piece(g)],
+                    fin_s.at[k - 1, g], fin_r.at[k - 1, g], down_y if k == 1 else up_y,
+                )
+
+    near_arrived(0)
     for g in range(4):
-        for k in (1, 2):
-            near[k, g].wait_recv()
-            if (k == 1) == (g < 2):
-                far.append(send(
-                    xbuf.at[core, k, piece(g)], xbuf.at[core, 3, piece(g)], fwd_s.at[g], fwd_r.at[g],
-                    up_y if k == 1 else down_y,
-                ))
-            sib[k, g] = to_sibling(k, g)
-    for k in (1, 2):
-        for g in range(4):
-            sib[k, g].wait_recv()
-        parts.append(compute(k))
-    for g in range(4):
-        far[g].wait_recv()
+        for o in range(g * per_group, (g + 1) * per_group):
+            if o:
+                far_arrivals[o].wait_recv()
         sib[3, g] = to_sibling(3, g)
-
-    final = {}
-
-    def finish_near(k, g, extra=None):
-        value = reduce_part(k, g)
-        if extra is not None:
-            value += extra.astype(F32)
-        p_send[k, piece(g), :] = value.astype(BF)
-        final[k, g] = send(
-            p_send.at[k, piece(g)], (fin_b if k == 1 else fin_a).at[piece(g)],
-            fin_s.at[k - 1, g], fin_r.at[k - 1, g], down_y if k == 1 else up_y,
-        )
-
-    parts[0].wait()
-    parts[1].wait()
-    parts[2].wait()
-    for g in range(4):
-        finish_near(1 if g < 2 else 2, g)
-    home[...] = p_mine[0].astype(F32) + p_back[0].astype(F32)
+    for spot in range(4):
+        sib[1, spot].wait_recv()
+    first_product(1, 1)
+    parts[1] = second_product(1, 1)
+    near_arrived(1)
     for g in range(4):
         sib[3, g].wait_recv()
-    parts.append(compute(3))
+    first_product(3, 0)
+    finish_near(0)
+    for spot in range(4):
+        sib[2, spot].wait_recv()
+    first_product(2, 1)
+    parts[2] = second_product(2, 1)
+    parts[3] = second_product(3, 0)
+    finish_near(1)
+    parts[0].wait()
+    home[...] = reduce_part(0)
     parts[3].wait()
-    relay = []
-    for g in range(4):
-        p_send[3, piece(g), :] = reduce_part(3, g).astype(BF)
-        relay.append(send(
-            p_send.at[3, piece(g)], (rs_a if g < 2 else rs_b).at[pl.ds((g % 2) * group, group)],
-            rs_s.at[g], rs_r.at[g], up_y if g < 2 else down_y,
-        ))
-    for g in (0, 2, 1, 3):
-        relay[g].wait_recv()
-        source = rs_a if g < 2 else rs_b
-        finish_near(2 if g < 2 else 1, g, source[pl.ds((g % 2) * group, group), :])
+    p_mine[3] = reduce_part(3).astype(BF)
+    far_replies = [None] + [
+        send(
+            p_mine.at[3, block(o)], returned_far.at[block(o)], far_ret_s.at[o], far_ret_r.at[o], peer_back(o)
+        )
+        for o in range(1, n_ex)
+    ]
+    returned_far[block(0), :] = p_mine[3, block(0), :]
     replies = [None] * n_ex
-    for g in (2, 3, 0, 1):
-        final[1, g].wait_recv()
-        final[2, g].wait_recv()
-        total = home[piece(g), :] + fin_a[piece(g), :].astype(F32) + fin_b[piece(g), :].astype(F32)
-        outgoing_rows = total.astype(BF)
-        p_mine[0, piece(g), :] = outgoing_rows
-        for o in range(g * per_group, (g + 1) * per_group):
-            if o:
-                replies[o] = send(
-                    p_mine.at[0, block(o)], returned.at[block(o)], ret_s.at[o], ret_r.at[o], peer_back(o)
-                )
+
+    def reply(groups):
+        for g in groups:
+            final[1, g].wait_recv()
+            final[2, g].wait_recv()
+            total = home[piece(g), :] + fin_a[piece(g), :].astype(F32) + fin_b[piece(g), :].astype(F32)
+            p_mine[0, piece(g), :] = total.astype(BF)
+            for o in range(g * per_group, (g + 1) * per_group):
+                if o:
+                    replies[o] = send(
+                        p_mine.at[0, block(o)], returned.at[block(o)], ret_s.at[o], ret_r.at[o], peer_back(o)
+                    )
+
+    reply((0, 1))
+    for o in range(1, n_ex):
+        far_replies[o].wait_recv()
+    back_far = returned_far[...]
+    far_out[...] = (bdot(mix_far[0], back_far) + bdot(mix_far[1], back_far)).astype(BF)
+    far_home = send(far_out, far_in, far_s.at[4], far_r.at[4], far_same)
+
+    reply((2, 3))
     returned[block(0), :] = p_mine[0, block(0), :]
+    far_home.wait_recv()
     for o in range(1, n_ex):
         replies[o].wait_recv()
-    mix = []
-    for c in range(2):
-        high = gates[c].astype(BF)
-        low = (gates[c] - high.astype(F32)).astype(BF)
-        mix.append((high, low))
-
     back = returned[...]
-    ys = [bdot(high, back) + bdot(low, back) for high, low in mix]
+    y = bdot(mix[0], back) + bdot(mix[1], back) + far_in[...].astype(F32)
     is_first = core == 0
-    y_send[...] = jnp.where(is_first, ys[1], ys[0])
+    y_send[...] = jnp.where(is_first, y[tokens:], y[:tokens])
     swap = send(y_send, y_back, pair_s.at[2], pair_r.at[2], sibling)
-    own_y = jnp.where(is_first, ys[0], ys[1])
-    residual[:, at_half] = residual[:, at_half] + own_y
+    residual[:, at_half] = residual[:, at_half] + jnp.where(is_first, y[:tokens], y[tokens:])
     swap.wait_recv()
     at_other = pl.ds(pl.multiple_of((1 - core) * half, half), half)
     residual[:, at_other] = residual[:, at_other] + y_back[...]
     for t in range(steps):
         out_ref[t] = residual[t * rows:(t + 1) * rows, :].astype(BF)
-    parts_done = {id(p) for p in parts}
+    waited = {id(p) for p in parts.values()}
     for copy in started:
-        if id(copy) not in parts_done:
+        if id(copy) not in waited:
             copy.wait_send()
 
 
@@ -700,28 +748,33 @@
             pltpu.VMEM((tokens, width), F32),
             pltpu.VMEM((2 * tokens, width), BF),
             pltpu.VMEM((steps, 2, rows), jnp.int32),
-            pltpu.VMEM((2, tokens, 128), jnp.int32),
+            pltpu.VMEM((2, tokens, 128), F32),
+            pltpu.VMEM((2, tokens, 128), F32),
             pltpu.VMEM((n_ex, width), BF),
             pltpu.VMEM((width, hidden_units), BF),
             pltpu.VMEM((hidden_units, width), BF),
+            pltpu.VMEM((2 * tokens, half), BF),
+            pltpu.VMEM((chunk_slots, half), BF),
             pltpu.VMEM((chunk_slots, half), BF),
             pltpu.VMEM((2, 4, chunk_slots, half), BF),
-            pltpu.VMEM((chunk_slots, hidden_units), BF),
+            pltpu.VMEM((2, chunk_slots, hidden_units), BF),
             pltpu.VMEM((4, chunk_slots, half), BF),
             pltpu.VMEM((4, chunk_slots, half), BF),
             pltpu.VMEM((4, chunk_slots, half), BF),
-            pltpu.VMEM((chunk_slots // 2, half), BF),
-            pltpu.VMEM((chunk_slots // 2, half), BF),
             pltpu.VMEM((chunk_slots, half), BF),
             pltpu.VMEM((chunk_slots, half), BF),
             pltpu.VMEM((chunk_slots, half), F32),
             pltpu.VMEM((chunk_slots, half), BF),
+            pltpu.VMEM((chunk_slots, half), BF),
+            pltpu.VMEM((2 * tokens, half), BF),
+            pltpu.VMEM((2 * tokens, half), BF),
             pltpu.VMEM((tokens, half), F32),
             pltpu.VMEM((tokens, half), F32),
-            dma((4,)), dma((3,)), dma((3,)), dma((n_ex,)), dma((n_ex,)), dma((2, 4)), dma((2, 4)),
-            dma((4,)), dma((4,)), dma((4, 4)), dma((4, 4)), dma((4,)), dma((4,)),
-            dma((4,)), dma((4,)), dma((2, 4)), dma((2, 4)), dma((n_ex,)), dma((n_ex,)),
-        ]
+            dma((4,)), dma((3,)), dma((3,)), dma((5,)), dma((5,)), dma((n_ex,)), dma((n_ex,)),
+            dma((n_ex,)), dma((n_ex,)), dma((2, 4)), dma((2, 4)), dma((4, 4)), dma((4, 4)), dma((4,)), dma((4,)),
+            dma((2, 4)), dma((2, 4)), dma((n_ex,)), dma((n_ex,)), dma((n_ex,)), dma((n_ex,)),
+    ]
+
     def kernel(*refs):
         layer_kernel(
             n_dp, n_ex, cap, refs[13:17],

time: 87.9 us -> 81.6 us (0.928)
  Pallas kernels: 86.3 us -> 79.9 us
    pallas_call x1, Pallas kernels: 86.3 us -> 79.9 us  [layer(): pl.pallas_call(kernel, out_shape=jax.ShapeDtypeStruct((steps, rows, width...]
where the time goes in v4:
time: 81.6 us; the launch traced here: 81.5 us
  Pallas kernels  79.9 us (98%)
  local copies, waits for them, and re-layouts  1.57 us (2%)
    pallas_call x1, Pallas kernels, layer(): pl.pallas_call(kernel, out_shape=jax.ShapeDtypeStruct((steps, rows, width...  79.9 us

profile of v4, /device:TPU:1, one launch (start us, length us, event | category | flops | bytes accessed | tf_op | source)
XLA Modules:
  0.0 81.5 jit_solution(14536780729606133524)
XLA Ops:
  0.0 79.9 %shard_map.163 = bf16[2,16,2048]{2,1,0:T(8,128)(2,1)} custom-call(bf16[2,16,2048]{2,1,0:T(8,128)(2,1)} %refs_0_.1, bf16[2,16,2048]{2,1,0:T(8,128)(2,1)} %refs_1_.1, bf16[2,16,2048]{2,1,0:T(8,128)(2,1)} %refs_2_.1, bf16[2,16,2048]{2,1,0:T(8,128)(2,1)} %refs_3_.1, bf16[2,16,2048]{2,1,0:T(8,128)(2,1)} %refs_4_.1, s32[2,16]{1,0:T(2,128)} %refs_5_.1, ...), custom_call_target="tpu_custom_call" | custom-call | tf_op jit(solution)/shard_map/pallas_call | solution.py:784
  79.9 1.6 %copy.19 = bf16[2,16,2048]{2,1,0:T(8,128)(2,1)} copy(bf16[2,16,2048]{2,1,0:T(8,128)(2,1)} %shard_map.163) | data formatting | bytes 262144

commit v5 on v4

--- a/solution.py
+++ b/solution.py
@@ -48,7 +48,7 @@
     return lax.dot_general(a, b, (((1,), (1,)), ((), ())), preferred_element_type=F32)
 
 
-def attention_part(n_dp, n_ex, rows, cache, src, beams, chunks, inputs, scratch, residual, normed, first_row, enter):
+def attention_part(n_dp, n_ex, rows, cache, src, beams, chunks, inputs, scratch, residual, normed, first_row, enter, tell, prepare):
     (
         hidden_hbm, q_self_hbm, k_new_hbm, v_new_hbm, q_cross_hbm, parents_hbm, ks_hbm, vs_hbm, gain_hbm,
         ck_hbm, cv_hbm, xk_hbm, xv_hbm,
@@ -140,6 +140,7 @@
     enter()
     for copy in out_copies:
         copy.start()
+    sent = tell()
 
     small[4].wait()
     small[5].wait()
@@ -294,6 +295,7 @@
     for copy in back_copies:
         copy.start()
 
+    prepare(sent)
     lax.fori_loop(early, chunks, cross_chunk, 0)
 
     for copy in back_copies:
@@ -367,10 +369,10 @@
 ):
     ids_hbm, router_hbm, w_in_hbm, w_out_hbm = inputs
     (
-        residual, normed, ids, info, info_far, router, w_in, w_out, normed_far, outgoing, outgoing_far,
+        residual, normed, ids, told, told_far, hot, dispatch, info, info_far, router, w_in, w_out, normed_far, outgoing, outgoing_far,
         xbuf, units, p_mine, p_send, p_back, fin_a, fin_b, home, returned, returned_far,
         far_out, far_in, y_send, y_back,
-        load_sem, pair_s, pair_r, far_s, far_r, a2a_s, a2a_r, far_a2a_s, far_a2a_r, near_s, near_r, sib_s, sib_r,
+        load_sem, ids_s, ids_r, pair_s, pair_r, far_s, far_r, a2a_s, a2a_r, far_a2a_s, far_a2a_r, near_s, near_r, sib_s, sib_r,
         part_s, part_r, fin_s, fin_r, ret_s, ret_r, far_ret_s, far_ret_r,
     ) = scratch
     steps, rows = ids.shape[0], ids.shape[2]
@@ -421,12 +423,13 @@
         pltpu.make_async_copy(w_out_hbm, w_out, load_sem.at[3]),
     ]
 
+    for copy in loads[:2]:
+        copy.start()
+
     def enter():
-        for copy in loads:
+        for copy in loads[2:]:
             copy.start()
         pl.semaphore_wait(barrier, len(others))
-
-    attention_part(n_dp, n_ex, *attention_args, residual, normed, mine, enter)
 
     started = []
 
@@ -439,6 +442,57 @@
         started.append(copy)
         return copy
 
+    def from_far(source, target, s_sem, r_sem):
+        return pltpu.make_async_remote_copy(
+            src_ref=source, dst_ref=target, send_sem=s_sem, recv_sem=r_sem,
+            device_id=far_same, device_id_type=MESH,
+        )
+
+    lane_i = iota((tokens, 128), 1)
+
+    def tell():
+        loads[0].wait()
+        named = [
+            jnp.concatenate([as_column(ids[t, k:k + 1, :].astype(F32), rows) for t in range(steps)], axis=0)
+            for k in range(2)
+        ]
+        told[core] = jnp.where(lane_i == 0, named[0], named[1])
+        sent = [send(told.at[core], told.at[core], ids_s.at[0], ids_r.at[0], sibling)]
+        for c in range(2):
+            sent.append(send(told.at[core], told_far.at[core], ids_s.at[1 + c], ids_r.at[1 + core], (far_place + c, me)))
+        return sent
+
+    def prepare(sent):
+        sent[0].wait_recv()
+        for c in range(2):
+            from_far(told.at[core], told_far.at[c], ids_s.at[1 + c], ids_r.at[1 + c]).wait_recv()
+        lane_x = lane_i.astype(F32)
+        lower = (iota((tokens, tokens), 1) < iota((tokens, tokens), 0)) & (
+            iota((tokens, tokens), 0) // rows == iota((tokens, tokens), 1) // rows
+        )
+        lower = jnp.where(lower, 1.0, 0.0).astype(BF)
+        step_of = (iota((tokens, 1), 0) // rows).astype(F32)
+        lane_c = iota((tokens, chunk), 1).astype(F32)
+        my_expert = me.astype(F32)
+        for which, table in enumerate((told, told_far)):
+            either = []
+            for c in range(2):
+                named = [table[c, :, k:k + 1] for k in range(2)]
+                one_hot = [lane_x == n for n in named]
+                before = bdot(lower, jnp.where(one_hot[0] | one_hot[1], 1.0, 0.0).astype(BF))
+                hots = []
+                for k in range(2):
+                    spot = jnp.sum(jnp.where(one_hot[k], before, 0.0), axis=1, keepdims=True)
+                    distance = named[k] - my_expert
+                    distance = jnp.where(distance < 0.0, distance + n_ex, distance)
+                    column = distance * slots + spot + step_of * cap + c * steps * cap
+                    hots.append(jnp.where(lane_c == column, 1.0, 0.0))
+                    hot[which, k, c * tokens:(c + 1) * tokens, :] = hots[k]
+                either.append(hots[0] + hots[1])
+            dispatch[which] = jnp.concatenate(either, axis=0).T.astype(BF)
+
+    attention_part(n_dp, n_ex, *attention_args, residual, normed, mine, enter, tell, prepare)
+
     pair = [send(normed.at[mine], normed.at[mine], pair_s.at[0], pair_r.at[0], sibling)]
     far = [
         send(
@@ -447,53 +501,22 @@
         for c in range(2)
     ]
 
-    loads[0].wait()
     loads[1].wait()
     logits = tdot(normed[mine, :], router[...])
     lane_e = iota((tokens, n_ex), 1).astype(F32)
-    lane_i = iota((tokens, 128), 1)
-    named = [
-        jnp.concatenate([as_column(ids[t, k:k + 1, :].astype(F32), rows) for t in range(steps)], axis=0)
-        for k in range(2)
-    ]
-    picked = [jnp.sum(jnp.where(lane_e == n, logits, 0.0), axis=1, keepdims=True) for n in named]
-    first_gate = 1.0 / (1.0 + jnp.exp(picked[1] - picked[0]))
-    info[core] = jnp.where(lane_i == 0, named[0], jnp.where(lane_i == 1, named[1], first_gate))
+    picked = [
+        jnp.sum(jnp.where(lane_e == told[core, :, k:k + 1], logits, 0.0), axis=1, keepdims=True) for k in range(2)
+    ]
+    info[core] = 1.0 / (1.0 + jnp.exp(picked[1] - picked[0])) + jnp.zeros((tokens, 128), F32)
     pair.append(send(info.at[core], info.at[core], pair_s.at[1], pair_r.at[1], sibling))
     for c in range(2):
         far.append(send(info.at[core], info_far.at[core], far_s.at[2 + c], far_r.at[2 + core], (far_place + c, me)))
 
-    lane_x = iota((tokens, 128), 1).astype(F32)
-    lower = (iota((tokens, tokens), 1) < iota((tokens, tokens), 0)) & (
-        iota((tokens, tokens), 0) // rows == iota((tokens, tokens), 1) // rows
-    )
-    lower = jnp.where(lower, 1.0, 0.0).astype(BF)
-    step_of = (iota((tokens, 1), 0) // rows).astype(F32)
-    lane_c = iota((tokens, chunk), 1).astype(F32)
-    my_expert = me.astype(F32)
-
-    def routes(table):
-        hot_rows, gate_rows = [], []
-        for c in range(2):
-            named = [table[c, :, k:k + 1] for k in range(2)]
-            gate = table[c, :, 2:3]
-            one_hot = [lane_x == n for n in named]
-            before = bdot(lower, jnp.where(one_hot[0] | one_hot[1], 1.0, 0.0).astype(BF))
-            hots = []
-            for k in range(2):
-                spot = jnp.sum(jnp.where(one_hot[k], before, 0.0), axis=1, keepdims=True)
-                distance = named[k] - my_expert
-                distance = jnp.where(distance < 0.0, distance + n_ex, distance)
-                column = distance * slots + spot + step_of * cap + c * steps * cap
-                hots.append(lane_c == column)
-            hot_rows.append(jnp.where(hots[0] | hots[1], 1.0, 0.0).astype(BF))
-            gate_rows.append(jnp.where(hots[0], gate, 0.0) + jnp.where(hots[1], 1.0 - gate, 0.0))
-        gates = jnp.concatenate(gate_rows, axis=0)
+    def mixed(which, table, back):
+        gate = jnp.concatenate([table[c, :, 0:1] for c in range(2)], axis=0)
+        gates = hot[which, 0] * gate + hot[which, 1] * (1.0 - gate)
         high = gates.astype(BF)
-        return jnp.concatenate(hot_rows, axis=0), (high, (gates - high.astype(F32)).astype(BF))
-
-    def spread(hot, value):
-        return lax.dot_general(hot, value, (((0,), (0,)), ((), ())), preferred_element_type=F32).astype(BF)
+        return bdot(high, back) + bdot((gates - high.astype(F32)).astype(BF), back)
 
     def block(o):
         return pl.ds(o * slots, slots)
@@ -502,32 +525,18 @@
         return pl.ds(g * group, group)
 
     at_half = pl.ds(pl.multiple_of(core * half, half), half)
-    for copy in pair:
-        copy.wait_recv()
-    dispatch, mix = routes(info)
-    outgoing[...] = spread(dispatch, normed[:, at_half])
+    pair[0].wait_recv()
+    outgoing[...] = bdot(dispatch[0], normed[:, at_half]).astype(BF)
     arrivals = [None] + [
         send(outgoing.at[block(o)], xbuf.at[core, 0, block(o)], a2a_s.at[o], a2a_r.at[o], peer(o))
         for o in range(1, n_ex)
     ]
     xbuf[core, 0, block(0), :] = outgoing[block(0), :]
-    recv_far = [
-        pltpu.make_async_remote_copy(
-            src_ref=normed.at[mine, pl.ds(0, half)], dst_ref=normed_far.at[pl.ds(c * tokens, tokens)],
-            send_sem=far_s.at[c], recv_sem=far_r.at[c], device_id=far_same, device_id_type=MESH,
-        )
-        for c in range(2)
-    ] + [
-        pltpu.make_async_remote_copy(
-            src_ref=info.at[core], dst_ref=info_far.at[c],
-            send_sem=far_s.at[2 + c], recv_sem=far_r.at[2 + c], device_id=far_same, device_id_type=MESH,
-        )
-        for c in range(2)
-    ]
-    for copy in recv_far:
-        copy.wait_recv()
-    dispatch_far, mix_far = routes(info_far)
-    outgoing_far[...] = spread(dispatch_far, normed_far[...])
+    for c in range(2):
+        from_far(
+            normed.at[mine, pl.ds(0, half)], normed_far.at[pl.ds(c * tokens, tokens)], far_s.at[c], far_r.at[c]
+        ).wait_recv()
+    outgoing_far[...] = bdot(dispatch[1], normed_far[...]).astype(BF)
     far_arrivals = [None] + [
         send(outgoing_far.at[block(o)], xbuf.at[core, 3, block(o)], far_a2a_s.at[o], far_a2a_r.at[o], peer(o))
         for o in range(1, n_ex)
@@ -625,15 +634,10 @@
     for g in range(4):
         sib[3, g].wait_recv()
     first_product(3, 0)
+    parts[3] = second_product(3, 0)
     finish_near(0)
     for spot in range(4):
         sib[2, spot].wait_recv()
-    first_product(2, 1)
-    parts[2] = second_product(2, 1)
-    parts[3] = second_product(3, 0)
-    finish_near(1)
-    parts[0].wait()
-    home[...] = reduce_part(0)
     parts[3].wait()
     p_mine[3] = reduce_part(3).astype(BF)
     far_replies = [None] + [
@@ -643,6 +647,11 @@
         for o in range(1, n_ex)
     ]
     returned_far[block(0), :] = p_mine[3, block(0), :]
+    first_product(2, 1)
+    parts[2] = second_product(2, 1)
+    finish_near(1)
+    parts[0].wait()
+    home[...] = reduce_part(0)
     replies = [None] * n_ex
 
     def reply(groups):
@@ -657,20 +666,22 @@
                         p_mine.at[0, block(o)], returned.at[block(o)], ret_s.at[o], ret_r.at[o], peer_back(o)
                     )
 
-    reply((0, 1))
+    reply((0, 1, 2, 3))
     for o in range(1, n_ex):
         far_replies[o].wait_recv()
     back_far = returned_far[...]
-    far_out[...] = (bdot(mix_far[0], back_far) + bdot(mix_far[1], back_far)).astype(BF)
+    for c in range(2):
+        from_far(info.at[core], info_far.at[c], far_s.at[2 + c], far_r.at[2 + c]).wait_recv()
+    far_out[...] = mixed(1, info_far, back_far).astype(BF)
     far_home = send(far_out, far_in, far_s.at[4], far_r.at[4], far_same)
 
-    reply((2, 3))
     returned[block(0), :] = p_mine[0, block(0), :]
     far_home.wait_recv()
     for o in range(1, n_ex):
         replies[o].wait_recv()
     back = returned[...]
-    y = bdot(mix[0], back) + bdot(mix[1], back) + far_in[...].astype(F32)
+    pair[1].wait_recv()
+    y = mixed(0, info, back) + far_in[...].astype(F32)
     is_first = core == 0
     y_send[...] = jnp.where(is_first, y[tokens:], y[:tokens])
     swap = send(y_send, y_back, pair_s.at[2], pair_r.at[2], sibling)
@@ -750,6 +761,10 @@
             pltpu.VMEM((steps, 2, rows), jnp.int32),
             pltpu.VMEM((2, tokens, 128), F32),
             pltpu.VMEM((2, tokens, 128), F32),
+            pltpu.VMEM((2, 2, 2 * tokens, chunk_slots), F32),
+            pltpu.VMEM((2, chunk_slots, 2 * tokens), BF),
+            pltpu.VMEM((2, tokens, 128), F32),
+            pltpu.VMEM((2, tokens, 128), F32),
             pltpu.VMEM((n_ex, width), BF),
             pltpu.VMEM((width, hidden_units), BF),
             pltpu.VMEM((hidden_units, width), BF),
@@ -770,7 +785,7 @@
             pltpu.VMEM((2 * tokens, half), BF),
             pltpu.VMEM((tokens, half), F32),
             pltpu.VMEM((tokens, half), F32),
-            dma((4,)), dma((3,)), dma((3,)), dma((5,)), dma((5,)), dma((n_ex,)), dma((n_ex,)),
+            dma((4,)), dma((3,)), dma((3,)), dma((3,)), dma((3,)), dma((5,)), dma((5,)), dma((n_ex,)), dma((n_ex,)),
             dma((n_ex,)), dma((n_ex,)), dma((2, 4)), dma((2, 4)), dma((4, 4)), dma((4, 4)), dma((4,)), dma((4,)),
             dma((2, 4)), dma((2, 4)), dma((n_ex,)), dma((n_ex,)), dma((n_ex,)), dma((n_ex,)),
     ]

time: 81.6 us -> 79.3 us (0.972)
  Pallas kernels: 79.9 us -> 77.6 us
    pallas_call x1, Pallas kernels: 79.9 us -> 77.6 us  [layer(): pl.pallas_call(kernel, out_shape=jax.ShapeDtypeStruct((steps, rows, width...]
where the time goes in v5:
time: 79.3 us; the launch traced here: 79.1 us
  Pallas kernels  77.6 us (98%)
  local copies, waits for them, and re-layouts  1.57 us (2%)
    pallas_call x1, Pallas kernels, layer(): pl.pallas_call(kernel, out_shape=jax.ShapeDtypeStruct((steps, rows, width...  77.6 us

profile of v5, /device:TPU:1, one launch (start us, length us, event | category | flops | bytes accessed | tf_op | source)
XLA Modules:
  0.0 79.1 jit_solution(4133609222018919607)
XLA Ops:
  0.0 77.6 %shard_map.163 = bf16[2,16,2048]{2,1,0:T(8,128)(2,1)} custom-call(bf16[2,16,2048]{2,1,0:T(8,128)(2,1)} %refs_0_.1, bf16[2,16,2048]{2,1,0:T(8,128)(2,1)} %refs_1_.1, bf16[2,16,2048]{2,1,0:T(8,128)(2,1)} %refs_2_.1, bf16[2,16,2048]{2,1,0:T(8,128)(2,1)} %refs_3_.1, bf16[2,16,2048]{2,1,0:T(8,128)(2,1)} %refs_4_.1, s32[2,16]{1,0:T(2,128)} %refs_5_.1, ...), custom_call_target="tpu_custom_call" | custom-call | tf_op jit(solution)/shard_map/pallas_call | solution.py:799
  77.6 1.6 %copy.19 = bf16[2,16,2048]{2,1,0:T(8,128)(2,1)} copy(bf16[2,16,2048]{2,1,0:T(8,128)(2,1)} %shard_map.163) | data formatting | bytes 262144

commit v6 on v5

--- a/solution.py
+++ b/solution.py
@@ -553,7 +553,7 @@
     def from_near(k, g):
         return 1 + g // 2, 2 * (k - 1) + g % 2
 
-    tile = min(256, half, hidden_units)
+    tile = min(1024, half, hidden_units)
 
     def first_product(k, slot):
         def first(j, carry):

time: 79.3 us -> 74.4 us (0.938)
  Pallas kernels: 77.6 us -> 72.7 us
    pallas_call x1, Pallas kernels: 77.6 us -> 72.7 us  [layer(): pl.pallas_call(kernel, out_shape=jax.ShapeDtypeStruct((steps, rows, width...]
where the time goes in v6:
time: 74.4 us; the launch traced here: 74.2 us
  Pallas kernels  72.7 us (98%)
  local copies, waits for them, and re-layouts  1.57 us (2%)
    pallas_call x1, Pallas kernels, layer(): pl.pallas_call(kernel, out_shape=jax.ShapeDtypeStruct((steps, rows, width...  72.7 us
    unnamed x1, local copies, waits for them, and re-layouts  1.57 us

profile of v6, /device:TPU:1, one launch (start us, length us, event | category | flops | bytes accessed | tf_op | source)
XLA Modules:
  0.0 74.2 jit_solution(15693580999087495312)
XLA Ops:
  0.0 72.7 %shard_map.163 = bf16[2,16,2048]{2,1,0:T(8,128)(2,1)} custom-call(bf16[2,16,2048]{2,1,0:T(8,128)(2,1)} %refs_0_.1, bf16[2,16,2048]{2,1,0:T(8,128)(2,1)} %refs_1_.1, bf16[2,16,2048]{2,1,0:T(8,128)(2,1)} %refs_2_.1, bf16[2,16,2048]{2,1,0:T(8,128)(2,1)} %refs_3_.1, bf16[2,16,2048]{2,1,0:T(8,128)(2,1)} %refs_4_.1, s32[2,16]{1,0:T(2,128)} %refs_5_.1, ...), custom_call_target="tpu_custom_call" | custom-call | tf_op jit(solution)/shard_map/pallas_call | solution.py:799
  72.7 1.6 %copy.19 = bf16[2,16,2048]{2,1,0:T(8,128)(2,1)} copy(bf16[2,16,2048]{2,1,0:T(8,128)(2,1)} %shard_map.163) | data formatting | bytes 262144
